TPU v7x, 512 devices: a whole 4x8x8 slice. The times are simulated.
512 devices in a mesh: feat: 32 (over z, x), rep: 16 (over y, core).
Axes of the slice: x: 4, y: 8, z: 8, core: 2. Of those that a mesh axis runs over, the one named last changes fastest.
Arguments:
- feature_table: bfloat16 [128, 16384], P('feat'), may hold values from -6 to 6
- node_ids: int32 [16, 6144], P('rep'), may hold values from 0 to 16383
- block_ids: int32 [16, 32, 4], P('rep'), may hold values from 0 to 47, as said below
- block_counts: int32 [16, 32], P('rep'), may hold values from 1 to 4, as said below
- adjacency: bfloat16 [16, 32, 4, 128, 128], P('rep'), may hold values from -0.25 to 0.25
- self_weight: bfloat16 [128, 256], replicated, may hold values from -0.375 to 0.375
- neigh_weight: bfloat16 [128, 256], replicated, may hold values from -0.375 to 0.375
- bias_vector: float32 [256], replicated, may hold values from -4 to 4
- cotangent: bfloat16 [16, 4096, 256], P('rep', 'feat'), may hold values from -6 to 6
Outputs:
- hidden: bfloat16 [16, 4096, 256], P('rep', 'feat')
- feature_grad: bfloat16 [16, 128, 6144], P('rep', 'feat')
- self_weight_grad: float32 [128, 256], replicated
- neigh_weight_grad: float32 [128, 256], replicated
- bias_grad: float32 [256], replicated
Inputs may be any that keep to these rules, and one draw needn't show every extreme that they name: `block_ids`: the 4 entries of a destination block's list are distinct source blocks, including unused slots. `block_counts`: in every replica some destination block uses all 4 slots.
All inputs are finite; a program needn't handle non-finite values.
Results may differ from a plain program's by a relative error of at most 0.0075.
Values may be sent and summed in bfloat16 or wider, within the bound.
No kernel may reach another device: no remote copies, remote signals or barrier semaphores. Data moves between devices by JAX's collectives and lax.ppermute only.
A program may use at most 64 MiB of HBM per device.

v0:
```python
import jax
import jax.numpy as jnp
from jax import lax
from jax.sharding import PartitionSpec as P


def aggregate_blocks(feature_cols, chosen_ids, chosen_adj, chosen_alive, block_side):
    chans = feature_cols.shape[0]
    source_count = feature_cols.shape[1] // block_side
    picked = jnp.take(feature_cols.reshape(chans, source_count, block_side), chosen_ids, axis=1)
    picked = jnp.where(chosen_alive[None, :, :, None], picked, jnp.zeros_like(picked))
    summed = jnp.einsum("cbks,bksd->cbd", picked, chosen_adj, preferred_element_type=jnp.float32)
    return summed.reshape(chans, -1).astype(jnp.bfloat16)


def spread_back(grad_cols, chosen_adj, chosen_onehot, block_side):
    chans = grad_cols.shape[0]
    block_count = chosen_adj.shape[0]
    contrib = jnp.einsum(
        "cbd,bksd->cbks",
        grad_cols.reshape(chans, block_count, block_side),
        chosen_adj,
        preferred_element_type=jnp.float32,
    )
    spread = jnp.einsum("cbks,bkn->cns", contrib, chosen_onehot, precision=lax.Precision.HIGHEST)
    return spread.reshape(chans, -1)


def local(
    feature_table,
    node_ids,
    block_ids,
    block_counts,
    adjacency,
    self_weight,
    neigh_weight,
    bias_vector,
    cotangent,
):
    features = jnp.take(feature_table, node_ids[0], axis=1)
    node_count = features.shape[1]
    blocks_all = adjacency.shape[1]
    list_depth = adjacency.shape[2]
    block_side = adjacency.shape[3]
    source_count = node_count // block_side
    dest_rows = blocks_all * block_side
    groups = lax.axis_size("feat")
    own_blocks = blocks_all // groups
    own_rows = own_blocks * block_side
    source_ids = block_ids[0]
    counts = block_counts[0]
    weights_all = adjacency[0]
    alive_mask = lax.broadcasted_iota(jnp.int32, (blocks_all, list_depth), 1) < counts[:, None]
    onehot = (
        (
            source_ids[:, :, None]
            == lax.broadcasted_iota(jnp.int32, (blocks_all, list_depth, source_count), 2)
        )
        & alive_mask[:, :, None]
    ).astype(jnp.float32)
    agg_cols = aggregate_blocks(features, source_ids, weights_all, alive_mask, block_side)
    stacked = jnp.stack([features[:, :dest_rows], agg_cols])
    arrived = lax.all_to_all(stacked, "feat", split_axis=2, concat_axis=1, tiled=True)
    self_rows = arrived[0]
    neigh_rows = arrived[1]
    contract_first = (((0,), (0,)), ((), ()))
    preact = lax.dot_general(
        self_rows, self_weight, contract_first, preferred_element_type=jnp.float32
    )
    preact = (
        preact
        + lax.dot_general(
            neigh_rows, neigh_weight, contract_first, preferred_element_type=jnp.float32
        )
        + bias_vector
    )
    sigmoid_v = jax.nn.sigmoid(preact)
    hidden = (preact * sigmoid_v).astype(jnp.bfloat16)
    grad_pre = (
        cotangent[0].astype(jnp.float32) * sigmoid_v * (1.0 + preact * (1.0 - sigmoid_v))
    ).astype(jnp.bfloat16)
    grad_self = jnp.dot(self_rows, grad_pre, preferred_element_type=jnp.float32)
    grad_neigh = jnp.dot(neigh_rows, grad_pre, preferred_element_type=jnp.float32)
    grad_bias = jnp.sum(grad_pre.astype(jnp.float32), axis=0)
    grad_self, grad_neigh, grad_bias = lax.psum((grad_self, grad_neigh, grad_bias), ("feat", "rep"))
    contract_last = (((1,), (1,)), ((), ()))
    agg_back = lax.dot_general(
        neigh_weight, grad_pre, contract_last, preferred_element_type=jnp.float32
    ).astype(jnp.bfloat16)
    self_back = lax.dot_general(
        self_weight, grad_pre, contract_last, preferred_element_type=jnp.float32
    ).astype(jnp.bfloat16)
    returned = lax.all_to_all(
        jnp.stack([self_back, agg_back]), "feat", split_axis=1, concat_axis=2, tiled=True
    )
    spread = spread_back(returned[1], weights_all, onehot, block_side)
    padded_self = jnp.pad(returned[0].astype(jnp.float32), ((0, 0), (0, node_count - dest_rows)))
    feature_grad = (spread + padded_self).astype(jnp.bfloat16)
    factor = float(own_rows * groups * lax.axis_size("rep")) ** (-0.5)
    return (
        hidden[None],
        feature_grad[None],
        grad_self * factor,
        grad_neigh * factor,
        grad_bias * factor,
    )


def solution(mesh):
    return jax.shard_map(
        local,
        mesh=mesh,
        in_specs=(
            P("feat", None),
            P("rep", None),
            P("rep", None, None),
            P("rep", None),
            P("rep", None, None, None, None),
            P(),
            P(),
            P(),
            P("rep", "feat", None),
        ),
        out_specs=(P("rep", "feat", None), P("rep", "feat", None), P(), P(), P()),
        check_vma=False,
    )
```

profile of v0, /device:TPU:1, one launch (start us, length us, event | category | flops | bytes accessed | tf_op | source)
XLA Modules:
  0.0 488.5 jit_solution(15687898559370783175)
XLA Ops:
  7.2 0.7 compare_and_fusion.2
  7.9 0.7 compare_select_fusion.3
  8.6 0.7 iota_compare_fusion.1
  9.5 0.8 compare_select_fusion
  10.2 0.8 compare_and_fusion
  11.0 0.8 compare_and_fusion.1
  12.0 4.1 copy.39
  16.0 19.2 %gather_fusion = bf16[6144,4]{1,0:T(8,128)(2,1)S(1)} fusion(bf16[4,16384]{0,1:T(8,128)(2,1)} %copy.39, s32[6144]{0:T(1024)S(1)} %broadcast_clamp_fusion), kind=kCustom, calls=%fused_computation | custom fusion | bytes 122880 | tf_op jit(solution)/shard_map/jit(_take)/gather | solution.py:40
  35.2 1.2 broadcast_select_fusion
  36.4 3.0 gather_fusion.1
  39.4 3.9 copy.43
  43.4 2.7 fusion.14
  46.1 0.5 copy.44
  46.7 2.2 fusion.19
  49.3 17.8 %copy.60 = bf16[2,4,4096]{1,0,2:T(2,128)(2,1)S(1)} copy(bf16[2,4,4096]{1,2,0:T(8,128)(2,1)S(1)} %pad_maximum_fusion) | data formatting | bytes 131072 | tf_op jit(solution)/shard_map/stack | solution.py:62
  67.1 4.0 reshape.178
  71.1 22.3 %all_to_all.30 = bf16[32,2,512]{2,1,0:T(2,128)(2,1)S(1)} all-to-all(bf16[32,2,512]{2,1,0:T(2,128)(2,1)S(1)} %reshape.178), channel_id=1, replica_groups=mesh['feat'=32,'rep'=16] {'feat'}, dimensions={0} | all-to-all | bytes 131072 | tf_op jit(solution)/shard_map/all_to_all | solution.py:63
  93.4 4.5 reshape.179
  97.9 2.4 copy.46
  100.6 0.9 convert_reduce_fusion
  101.8 0.8 fusion.44
  102.6 0.8 fusion.43
  103.4 97.4 %psum.23 = f32[256]{0:T(256)S(1)} all-reduce(f32[256]{0:T(256)S(1)} %get-tuple-element.7), channel_id=1, replica_groups=mesh['feat'=32,'rep'=16] {'feat','rep'}, use_global_device_ids=true, to_apply=%region_3.4 | all-reduce | flops 256 | bytes 2048 | tf_op jit(solution)/shard_map/psum | solution.py:85
  200.8 0.7 copy.47
  201.6 4.1 all-to-all-start.1
  205.7 0.7 all-reduce.4.cloned.1.call-update
  206.4 0.6 broadcast_multiply_fusion.2
  207.0 7.5 %all-to-all-done.1 = bf16[2,128,128]{2,0,1:T(2,128)(2,1)S(1)} async-done(((bf16[2,128,128]{2,0,1:T(2,128)(2,1)}), bf16[2,128,128]{2,0,1:T(2,128)(2,1)S(1)}, u32[]{:S(2)}, u32[]{:S(2)}) %all-to-all-start.1) | async-done | bytes 65568 | tf_op jit(solution)/shard_map/all_to_all | solution.py:93
  214.5 3.4 fusion.4
  218.3 0.7 fusion.35
  219.0 261.0 %all-reduce.4.cloned.1.call-done = (f32[128,256]{1,0:T(8,128)}, f32[128,256]{1,0:T(8,128)}) async-done(((f32[128,256]{1,0:T(8,128)}, f32[128,256]{1,0:T(8,128)}), (f32[128,256]{1,0:T(8,128)}, f32[128,256]{1,0:T(8,128)})) %all-reduce.4.cloned.1.call-update) | async-done | bytes 262160 | tf_op jit(solution)/shard_map/psum | solution.py:85
  480.0 1.7 broadcast_multiply_fusion
  (30 shorter events, 1.9 us)
Async XLA Ops:
  7.2 93.4 %copy-start = (bf16[128,256]{1,0:T(8,128)(2,1)S(1)}, bf16[128,256]{1,0:T(8,128)(2,1)}, u32[]{:S(2)}) copy-start(bf16[128,256]{1,0:T(8,128)(2,1)} %param.15) | copy-start | bytes 196612
  11.7 4.3 copy-start.3
  43.4 3.3 slice-start
  93.4 6.9 %copy-start.1 = (bf16[128,256]{1,0:T(8,128)(2,1)S(1)}, bf16[128,256]{1,0:T(8,128)(2,1)}, u32[]{:S(2)}) copy-start(bf16[128,256]{1,0:T(8,128)(2,1)} %param.14) | copy-start | bytes 196612
  93.4 7.1 %copy-start.4 = (bf16[1,128,256]{2,1,0:T(8,128)(2,1)S(1)}, bf16[1,128,256]{2,1,0:T(8,128)(2,1)}, u32[]{:S(2)}) copy-start(bf16[1,128,256]{2,1,0:T(8,128)(2,1)} %param.17) | copy-start | bytes 196612
  93.4 7.2 %copy-start.5 = (f32[256]{0:T(256)S(1)}, f32[256]{0:T(256)}, u32[]{:S(2)}) copy-start(f32[256]{0:T(256)} %param.16) | copy-start | bytes 3076
  201.6 12.9 %all-to-all-start.1 = ((bf16[2,128,128]{2,0,1:T(2,128)(2,1)}), bf16[2,128,128]{2,0,1:T(2,128)(2,1)S(1)}, u32[]{:S(2)}, u32[]{:S(2)}) async-start(bf16[2,128,128]{2,0,1:T(2,128)(2,1)} %copy.47), calls=%async_computation.1 | async-start | bytes 131072 | tf_op jit(solution)/shard_map/all_to_all | solution.py:93
  205.7 274.3 %all-reduce.4.cloned.1.call-start = ((), (), s32[]{:S(2)}) async-start(), calls=%async_computation.2 | async-start | bytes 524288 | tf_op jit(solution)/shard_map/psum | solution.py:85
  214.5 3.4 copy-start.2
Sparse Core Ops, SparseCore 0:
  212.3 267.6 all-reduce.3
where the time goes:
time: 489 us
  waiting for transfers between devices  269 us (55%)
  blocking collectives  120 us (25%)
  local copies, waits for them, and re-layouts  60.6 us (12%)
  between operations  14.3 us (3%)
  other arithmetic  11.1 us (2%)
  matrix products  9.47 us (2%)
    psum x1, waiting for transfers between devices, local(): lax.psum((grad_self, grad_neigh, grad_bias), ('feat', 'rep'))  261 us
    psum x1, blocking collectives, local(): lax.psum((grad_self, grad_neigh, grad_bias), ('feat', 'rep'))  97.4 us
    all_to_all x1, blocking collectives, local(): lax.all_to_all(stacked, 'feat', split_axis=2, concat_axis=1, tiled=True)  22.3 us
    gather x1, local copies, waits for them, and re-layouts, local(): features = jnp.take(feature_table, node_ids[0], axis=1)  19.2 us
    another operation x1, local copies, waits for them, and re-layouts, local(): stacked = jnp.stack([features[:, :dest_rows], agg_cols])  17.8 us
    unnamed x15, local copies, waits for them, and re-layouts  12.6 us
  transfers between devices with their start and end apart: 2, of which 2 were waited for; matrix products, arithmetic and copies ran while one was open for 1% of the time, Pallas kernels for 0%

commit v1 on v0

v1 whole, which is shorter than its diff:
```python
import jax
import jax.numpy as jnp
from jax import lax
from jax.experimental import pallas as pl
from jax.experimental.pallas import tpu as pltpu
from jax.sharding import PartitionSpec as P

F32 = jnp.float32
BF16 = jnp.bfloat16
ADJ_PARTS = 8
LOW = 256
CHUNK = 512


def adj_copies(adj_hbm, adj_vmem, sems):
    per = adj_vmem.shape[0] // ADJ_PARTS
    return [
        pltpu.make_async_copy(
            adj_hbm.at[0, pl.ds(p * per, per)], adj_vmem.at[pl.ds(p * per, per)], sems.at[p]
        )
        for p in range(ADJ_PARTS)
    ]


def forward_kernel(
    ids_ref, counts_ref, nodes_ref, table_ref, adj_hbm, out_ref, adj, rows_f32, feats, staged, sems
):
    copies = adj_copies(adj_hbm, adj, sems)
    for copy in copies:
        copy.start()
    chans = table_ref.shape[0]
    groups = table_ref.shape[1] // LOW
    for q in range(groups):
        rows_f32[q * chans : (q + 1) * chans, :] = table_ref[:, q * LOW : (q + 1) * LOW].astype(F32)
    table_rows = rows_f32[...].astype(BF16)
    node_count = nodes_ref.shape[1]
    for start in range(0, node_count, CHUNK):
        ids = nodes_ref[:, start : start + CHUNK]
        low = ids & (LOW - 1)
        high = ids // LOW
        onehot = jnp.where(lax.broadcasted_iota(jnp.int32, (LOW, CHUNK), 0) == low, 1.0, 0.0)
        spread = jnp.dot(table_rows, onehot.astype(BF16), preferred_element_type=F32)
        group = lax.broadcasted_iota(jnp.int32, spread.shape, 0) // chans
        kept = jnp.where(group == high, spread, 0.0)
        two = jnp.sum(kept.reshape(-1, 8, CHUNK), axis=0)
        both = two + pltpu.roll(two, 4, 0)
        for j in range(CHUNK // 128):
            feats[start // 128 + j] = both[:, j * 128 : (j + 1) * 128]
    blocks, depth = ids_ref.shape[1], ids_ref.shape[2]
    side = adj.shape[3]
    upper = lax.broadcasted_iota(jnp.int32, (8, side), 0) < chans
    per = blocks // ADJ_PARTS
    for b in range(blocks):
        if b % per == 0:
            copies[b // per].wait()
        count = counts_ref[0, b]
        picked = [
            jnp.where(k < count, feats[ids_ref[0, b, k]], 0.0) for k in range(depth)
        ]
        lhs = jnp.concatenate(picked, axis=1).astype(BF16)
        agg = jnp.dot(lhs, adj[b].reshape(depth * side, side), preferred_element_type=F32)
        staged[b] = jnp.where(upper, feats[b], agg)
    out_ref[...] = staged[...].astype(BF16)


def dense_kernel(x_ref, sw_ref, nw_ref, bias_ref, cot_ref, hidden_ref, send_ref):
    feats = sw_ref.shape[0]
    hid = sw_ref.shape[1]
    sw = sw_ref[...].astype(F32).reshape(feats // 8, 8, hid)
    nw = nw_ref[...].astype(F32).reshape(feats // 8, 8, hid)
    upper = lax.broadcasted_iota(jnp.int32, sw.shape, 1) < 4
    even = jnp.where(upper, sw, pltpu.roll(nw, 4, 1))
    odd = jnp.where(upper, pltpu.roll(sw, 4, 1), nw)
    weight = jnp.concatenate([even, odd], axis=1).reshape(2 * feats, hid).astype(BF16)
    rows = x_ref.shape[2]
    x = x_ref[...].reshape(2 * feats, rows)
    preact = lax.dot_general(x, weight, (((0,), (0,)), ((), ())), preferred_element_type=F32)
    preact = preact + bias_ref[...]
    sig = jax.nn.sigmoid(preact)
    hidden_ref[0] = (preact * sig).astype(BF16)
    grad_pre = (cot_ref[0].astype(F32) * sig * (1.0 + preact * (1.0 - sig))).astype(BF16)
    grads = jnp.dot(x, grad_pre, preferred_element_type=F32)
    back = lax.dot_general(
        weight, grad_pre, (((1,), (1,)), ((), ())), preferred_element_type=F32
    )
    bias_sum = jnp.sum(grad_pre.astype(F32), axis=0, keepdims=True)
    peers = x_ref.shape[0]
    half = hid // 2
    tail = split_rows(bias_sum[:, :half], bias_sum[:, half:])
    send_ref[...] = jnp.concatenate(
        [
            back.reshape(peers, 8, rows),
            grads[:, :half].reshape(peers, 8, half),
            grads[:, half:].reshape(peers, 8, half),
            jnp.broadcast_to(tail[None], (peers, 8, half)),
        ],
        axis=1,
    ).astype(BF16)


def split_rows(first, second):
    place = lax.broadcasted_iota(jnp.int32, (8, first.shape[1]), 0)
    first_hi = first.astype(BF16).astype(F32)
    second_hi = second.astype(BF16).astype(F32)
    out = jnp.where(place == 0, first_hi, 0.0)
    out = jnp.where(place == 1, second_hi, out)
    out = jnp.where(place == 2, first - first_hi, out)
    return jnp.where(place == 3, second - second_hi, out)


def feat_sum_kernel(got_ref, out_ref):
    total = jnp.sum(got_ref[...].astype(F32)[:, 8:, :], axis=0)
    low = total[16:24]
    tail = split_rows(low[0:1] + low[2:3], low[1:2] + low[3:4])
    whole = jnp.concatenate([total[:16], tail, jnp.zeros_like(tail)], axis=0).astype(BF16)
    out_ref[...] = jnp.broadcast_to(whole[None], out_ref.shape)


def rep_sum_kernel(factor, got_ref, out_ref, bias_ref):
    total = jnp.sum(got_ref[...].astype(F32), axis=0)
    low = total[16:24]
    bias_ref[...] = factor * jnp.concatenate([low[0:1] + low[2:3], low[1:2] + low[3:4]], axis=1)
    out_ref[...] = jnp.broadcast_to((factor * total[:16]).astype(BF16)[None], out_ref.shape)


def assemble_kernel(got_ref, self_ref, neigh_ref):
    peers = got_ref.shape[0]
    side = got_ref.shape[2]
    got = got_ref[...].astype(F32).reshape(peers // 2, 32, side)
    for h in range(2):
        even = got[:, 8 * h : 8 * h + 8]
        odd = got[:, 16 + 8 * h : 24 + 8 * h]
        upper = lax.broadcasted_iota(jnp.int32, even.shape, 1) < 4
        first = jnp.where(upper, even, pltpu.roll(odd, 4, 1))
        second = jnp.where(upper, pltpu.roll(even, 4, 1), odd)
        self_ref[:, h * side : (h + 1) * side] = first.reshape(peers * 4, side)
        neigh_ref[:, h * side : (h + 1) * side] = second.reshape(peers * 4, side)


def backward_kernel(ids_ref, counts_ref, got_ref, adj_hbm, out_ref, adj, acc, sems):
    copies = adj_copies(adj_hbm, adj, sems)
    for copy in copies:
        copy.start()
    acc[...] = jnp.zeros_like(acc)
    blocks, depth = ids_ref.shape[1], ids_ref.shape[2]
    side = adj.shape[3]
    sources = acc.shape[0] - 1
    per = blocks // ADJ_PARTS
    for b in range(blocks):
        if b % per == 0:
            copies[b // per].wait()
        count = counts_ref[0, b]
        lhs = got_ref[b, 0:16, :]
        contrib = lax.dot_general(
            lhs,
            adj[b].reshape(depth * side, side),
            (((1,), (1,)), ((), ())),
            preferred_element_type=F32,
        )
        for k in range(depth):
            place = jnp.where(k < count, ids_ref[0, b, k], sources)
            acc[place] = acc[place] + contrib[0:8, k * side : (k + 1) * side]
    chans = out_ref.shape[1]
    for n in range(sources):
        total = pltpu.roll(acc[n], 4, 0)
        if n < blocks:
            total = total + got_ref[n, 0:16, :].astype(F32)[0:8]
        out_ref[0, :, n * side : (n + 1) * side] = total[0:chans].astype(BF16)


SMEM = pl.BlockSpec(memory_space=pltpu.SMEM)
VMEM = pl.BlockSpec(memory_space=pltpu.VMEM)
HBM = pl.BlockSpec(memory_space=pltpu.HBM)


def params(mib):
    return pltpu.CompilerParams(vmem_limit_bytes=mib * 1024 * 1024)


def local(
    feature_table,
    node_ids,
    block_ids,
    block_counts,
    adjacency,
    self_weight,
    neigh_weight,
    bias_vector,
    cotangent,
):
    chans = feature_table.shape[0]
    node_count = node_ids.shape[1]
    blocks, depth, side = adjacency.shape[1:4]
    sources = node_count // side
    peers = lax.axis_size("feat")
    reps = lax.axis_size("rep")
    feats, hid = self_weight.shape
    rows = cotangent.shape[1]
    sent = pl.pallas_call(
        forward_kernel,
        out_shape=jax.ShapeDtypeStruct((peers, 8, side), BF16),
        in_specs=[SMEM, SMEM, VMEM, VMEM, HBM],
        out_specs=VMEM,
        scratch_shapes=[
            pltpu.VMEM(adjacency.shape[1:], BF16),
            pltpu.VMEM((feature_table.shape[1] // LOW * chans, LOW), F32),
            pltpu.VMEM((sources, 8, side), F32),
            pltpu.VMEM((peers, 8, side), F32),
            pltpu.SemaphoreType.DMA((ADJ_PARTS,)),
        ],
        compiler_params=params(24),
        name="forward",
    )(block_ids, block_counts, node_ids, feature_table, adjacency)
    arrived = lax.all_to_all(sent, "feat", split_axis=0, concat_axis=0, tiled=True)
    hidden, back = pl.pallas_call(
        dense_kernel,
        out_shape=(
            jax.ShapeDtypeStruct(cotangent.shape, BF16),
            jax.ShapeDtypeStruct((peers, 32, side), BF16),
        ),
        in_specs=[VMEM] * 5,
        out_specs=(VMEM, VMEM),
        compiler_params=params(24),
        name="dense",
    )(arrived, self_weight, neigh_weight, bias_vector.reshape(1, hid), cotangent)
    got = lax.all_to_all(back, "feat", split_axis=0, concat_axis=0, tiled=True)
    copies = pl.pallas_call(
        feat_sum_kernel,
        out_shape=jax.ShapeDtypeStruct((reps, 32, side), BF16),
        in_specs=[VMEM],
        out_specs=VMEM,
        name="feat_sum",
    )(got)
    over_rep = lax.all_to_all(copies, "rep", split_axis=0, concat_axis=0, tiled=True)
    feature_grad = pl.pallas_call(
        backward_kernel,
        out_shape=jax.ShapeDtypeStruct((1, chans, node_count), BF16),
        in_specs=[SMEM, SMEM, VMEM, HBM],
        out_specs=VMEM,
        scratch_shapes=[
            pltpu.VMEM(adjacency.shape[1:], BF16),
            pltpu.VMEM((sources + 1, 8, side), F32),
            pltpu.SemaphoreType.DMA((ADJ_PARTS,)),
        ],
        compiler_params=params(24),
        cost_estimate=pl.CostEstimate(
            flops=2 * 16 * adjacency.size, bytes_accessed=2 * adjacency.size, transcendentals=0
        ),
        name="spread_back",
    )(block_ids, block_counts, got, adjacency)
    factor = float(rows * peers * reps) ** (-0.5)
    pieces, bias_grad = pl.pallas_call(
        lambda *refs: rep_sum_kernel(factor, *refs),
        out_shape=(
            jax.ShapeDtypeStruct((peers, 16, side), BF16),
            jax.ShapeDtypeStruct((1, hid), F32),
        ),
        in_specs=[VMEM],
        out_specs=(VMEM, VMEM),
        name="rep_sum",
    )(over_rep)
    whole = lax.all_to_all(pieces, "feat", split_axis=0, concat_axis=0, tiled=True)
    self_grad, neigh_grad = pl.pallas_call(
        assemble_kernel,
        out_shape=(
            jax.ShapeDtypeStruct((feats, hid), F32),
            jax.ShapeDtypeStruct((feats, hid), F32),
        ),
        in_specs=[VMEM],
        out_specs=(VMEM, VMEM),
        name="assemble",
    )(whole)
    return hidden, feature_grad, self_grad, neigh_grad, bias_grad.reshape(hid)


def solution(mesh):
    return jax.shard_map(
        local,
        mesh=mesh,
        in_specs=(
            P("feat", None),
            P("rep", None),
            P("rep", None, None),
            P("rep", None),
            P("rep", None, None, None, None),
            P(),
            P(),
            P(),
            P("rep", "feat", None),
        ),
        out_specs=(P("rep", "feat", None), P("rep", "feat", None), P(), P(), P()),
        check_vma=False,
    )
```

time: 489 us -> 87.4 us (0.18)
  waiting for transfers between devices: 269 us -> 2.95 us
  blocking collectives: 120 us -> 56.5 us
  local copies, waits for them, and re-layouts: 60.6 us -> 9.07 us
  Pallas kernels: 0 us -> 13.7 us
  between operations: 14.3 us -> 0.71 us
  other arithmetic: 11.1 us -> 0 us
  matrix products: 9.47 us -> 0 us
    psum x1 -> x0, waiting for transfers between devices: 261 us -> none  [local(): lax.psum((grad_self, grad_neigh, grad_bias), ('feat', 'rep'))]
    psum x1 -> x0, blocking collectives: 97.4 us -> none  [local(): lax.psum((grad_self, grad_neigh, grad_bias), ('feat', 'rep'))]
    all_to_all x1 -> x3, blocking collectives: 22.3 us -> 56.5 us  [the longest x1 22.3 us: local(): lax.all_to_all(sent, 'feat', split_axis=0, concat_axis=0, tiled=True)]
    gather x3 -> x0, local copies, waits for them, and re-layouts: 26.2 us -> none  [the longest x1 19.2 us: local(): features = jnp.take(feature_table, node_ids[0], axis=1)]
    another operation x2 -> x0, local copies, waits for them, and re-layouts: 18.6 us -> none  [the longest x1 17.8 us: local(): stacked = jnp.stack([features[:, :dest_rows], agg_cols])]
    pallas_call x0 -> x6, Pallas kernels: none -> 13.7 us  [the longest x1 4.08 us: local(): pl.pallas_call(forward_kernel, out_shape=jax.ShapeDtypeStruct((peers, 8,...]
    dot_general x9 -> x0, matrix products: 9.47 us -> none  [the longest x1 3.37 us: spread_back(): jnp.einsum('cbd,bksd->cbks', grad_cols.reshape(chans, block_count, block_...]
    unnamed x15 -> x25, local copies, waits for them, and re-layouts: 12.6 us -> 9.07 us
  transfers between devices with their start and end apart: 2 -> 1, of which waited for: 2 -> 1; matrix products, arithmetic and copies ran while one was open for 1% -> 0% of each run, Pallas kernels for 0% -> 5%
where the time goes in v1:
time: 87.4 us; the launch traced here: 86.8 us
  blocking collectives  56.5 us (65%)
  Pallas kernels  13.7 us (16%)
  local copies, waits for them, and re-layouts  9.07 us (10%)
  starting transfers between devices  3.86 us (4%)
  waiting for transfers between devices  2.95 us (3%)
    all_to_all x1, blocking collectives, local(): lax.all_to_all(sent, 'feat', split_axis=0, concat_axis=0, tiled=True)  22.3 us
    all_to_all x1, blocking collectives, local(): lax.all_to_all(copies, 'rep', split_axis=0, concat_axis=0, tiled=True)  19.9 us
    all_to_all x1, blocking collectives, local(): got = lax.all_to_all(back, 'feat', split_axis=0, concat_axis=0, tiled=True)  14.2 us
    unnamed x25, local copies, waits for them, and re-layouts  9.07 us
    pallas_call x1, Pallas kernels, local(): pl.pallas_call(forward_kernel, out_shape=jax.ShapeDtypeStruct((peers, 8,...  4.08 us
    pallas_call x1, Pallas kernels, local(): pl.pallas_call(backward_kernel, out_shape=jax.ShapeDtypeStruct((1, chans,...  3.92 us
    all_to_all x1, starting transfers between devices, local(): lax.all_to_all(pieces, 'feat', split_axis=0, concat_axis=0, tiled=True)  3.86 us
    all_to_all x1, waiting for transfers between devices, local(): lax.all_to_all(pieces, 'feat', split_axis=0, concat_axis=0, tiled=True)  2.95 us
  transfers between devices with their start and end apart: 1, of which 1 were waited for; matrix products, arithmetic and copies ran while one was open for 0% of the time, Pallas kernels for 5%

profile of v1, /device:TPU:1, one launch (start us, length us, event | category | flops | bytes accessed | tf_op | source)
XLA Modules:
  0.0 86.8 jit_solution(15138362375710469082)
XLA Ops:
  0.6 0.0 copy-start.9
  0.6 0.0 copy-start.10
  0.7 0.8 copy.14.ids_ref
  1.4 0.0 copy-start
  1.4 2.2 %copy-done = bf16[1,32,4,128,128]{4,3,2,1,0:T(8,128)(2,1)S(1)} copy-done((bf16[1,32,4,128,128]{4,3,2,1,0:T(8,128)(2,1)S(1)}, bf16[1,32,4,128,128]{4,3,2,1,0:T(8,128)(2,1)}, u32[]{:S(2)}) %copy-start) | copy-done | bytes 4194328
  3.6 0.0 copy-start.3
  3.6 0.9 %copy-done.3 = bf16[4,16384]{1,0:T(4,128)(2,1)S(1)} copy-done((bf16[4,16384]{1,0:T(4,128)(2,1)S(1)}, bf16[4,16384]{1,0:T(4,128)(2,1)}, u32[]{:S(2)}) %copy-start.3) | copy-done | bytes 131096
  4.5 0.0 copy-start.7
  4.5 0.7 copy-done.7
  5.3 0.7 copy-done.8
  5.9 0.0 copy-start.4
  5.9 0.0 copy-start.5
  5.9 4.1 %forward.1 = bf16[32,8,128]{2,1,0:T(8,128)(2,1)S(1)} custom-call(s32[1,32,4]{2,1,0:T(8,128)S(1)} %copy.14.ids_ref, s32[1,32]{1,0:T(1,128)S(1)} %copy-done.8, s32[1,6144]{1,0:T(1,128)S(1)} %copy-done.7, bf16[4,16384]{1,0:T(4,128)(2,1)S(1)} %copy-done.3, bf16[1,32,4,128,128]{4,3,2,1,0:T(8,128)(2,1)S(1)} %copy-done), custom_call_target="tpu_custom_call" | custom-call | tf_op jit(solution)/shard_map/forward/pallas_call | solution.py:199
  10.0 22.3 %all_to_all.20.x_ref = bf16[32,8,128]{2,1,0:T(8,128)(2,1)S(1)} all-to-all(bf16[32,8,128]{2,1,0:T(8,128)(2,1)S(1)} %forward.1), channel_id=1, replica_groups=mesh['feat'=32,'rep'=16] {'feat'}, dimensions={0} | all-to-all | bytes 131072 | tf_op jit(solution)/shard_map/all_to_all | solution.py:214
  32.3 0.0 copy-done.10
  32.3 0.0 copy-done.4
  32.3 0.0 copy-done.5
  32.4 0.0 copy-done.6
  32.4 0.9 dense.1
  33.2 14.2 %all_to_all.21.got_ref = bf16[32,32,128]{2,1,0:T(8,128)(2,1)} all-to-all(bf16[32,32,128]{2,1,0:T(8,128)(2,1)S(1)} %get-tuple-element.12), channel_id=1, replica_groups=mesh['feat'=32,'rep'=16] {'feat'}, dimensions={0} | all-to-all | bytes 524288 | tf_op jit(solution)/shard_map/all_to_all | solution.py:226
  47.5 1.7 %feat_sum.1 = bf16[16,32,128]{2,1,0:T(8,128)(2,1)} custom-call(bf16[32,32,128]{2,1,0:T(8,128)(2,1)} %all_to_all.21.got_ref), custom_call_target="tpu_custom_call" | custom-call | tf_op jit(solution)/shard_map/feat_sum/pallas_call | solution.py:227
  49.1 19.9 %all_to_all.22.refs_0_ = bf16[16,32,128]{2,1,0:T(8,128)(2,1)} all-to-all(bf16[16,32,128]{2,1,0:T(8,128)(2,1)} %feat_sum.1), channel_id=1, replica_groups=mesh['feat'=32,'rep'=16] {'rep'}, dimensions={0} | all-to-all | bytes 262144 | tf_op jit(solution)/shard_map/all_to_all | solution.py:234
  69.0 1.6 %rep_sum.1 = (bf16[32,16,128]{2,1,0:T(8,128)(2,1)}, f32[1,256]{1,0:T(1,128)}) custom-call(bf16[16,32,128]{2,1,0:T(8,128)(2,1)} %all_to_all.22.refs_0_), custom_call_target="tpu_custom_call" | custom-call | tf_op jit(solution)/shard_map/rep_sum/pallas_call | solution.py:252
  70.6 3.9 %all-to-all-start.3 = ((bf16[32,16,128]{2,1,0:T(8,128)(2,1)}), bf16[32,16,128]{2,1,0:T(8,128)(2,1)S(1)}, u32[]{:S(2)}, u32[]{:S(2)}) async-start(bf16[32,16,128]{2,1,0:T(8,128)(2,1)} %get-tuple-element.13), calls=%async_computation.3 | async-start | bytes 262144 | tf_op jit(solution)/shard_map/all_to_all | solution.py:262
  74.5 0.0 copy-done.9
  74.5 0.0 copy-start.1
  74.5 2.2 %copy-done.1 = bf16[1,32,4,128,128]{4,3,2,1,0:T(8,128)(2,1)S(1)} copy-done((bf16[1,32,4,128,128]{4,3,2,1,0:T(8,128)(2,1)S(1)}, bf16[1,32,4,128,128]{4,3,2,1,0:T(8,128)(2,1)}, u32[]{:S(2)}) %copy-start.1) | copy-done | bytes 4194328
  76.7 0.9 %copy-done.2 = bf16[32,32,128]{2,1,0:T(8,128)(2,1)S(1)} copy-done((bf16[32,32,128]{2,1,0:T(8,128)(2,1)S(1)}, bf16[32,32,128]{2,1,0:T(8,128)(2,1)}, u32[]{:S(2)}) %copy-start.2) | copy-done | bytes 262168
  77.6 3.9 %spread_back.1 = bf16[1,4,6144]{2,1,0:T(4,128)(2,1)} custom-call(s32[1,32,4]{2,1,0:T(8,128)S(1)} %copy.14.ids_ref, s32[1,32]{1,0:T(1,128)S(1)} %copy-done.9, bf16[32,32,128]{2,1,0:T(8,128)(2,1)S(1)} %copy-done.2, bf16[1,32,4,128,128]{4,3,2,1,0:T(8,128)(2,1)S(1)} %copy-done.1), custom_call_target="tpu_custom_call" | custom-call | flops 67108864 | bytes 4194304 | tf_op jit(solution)/shard_map/spread_back/pallas_call | solution.py:235
  81.5 3.0 %all-to-all-done.3.got_ref = bf16[32,16,128]{2,1,0:T(8,128)(2,1)S(1)} async-done(((bf16[32,16,128]{2,1,0:T(8,128)(2,1)}), bf16[32,16,128]{2,1,0:T(8,128)(2,1)S(1)}, u32[]{:S(2)}, u32[]{:S(2)}) %all-to-all-start.3) | async-done | bytes 131104 | tf_op jit(solution)/shard_map/all_to_all | solution.py:262
  84.5 0.7 copy-done.11
  85.1 1.6 %assemble.1 = (f32[128,256]{1,0:T(8,128)}, f32[128,256]{1,0:T(8,128)}) custom-call(bf16[32,16,128]{2,1,0:T(8,128)(2,1)} %copy-done.11), custom_call_target="tpu_custom_call" | custom-call | tf_op jit(solution)/shard_map/assemble/pallas_call | solution.py:263
  (4 shorter events, 0.0 us)
Async XLA Ops:
  0.6 73.8 %copy-start.9 = (s32[1,32]{1,0:T(1,128)S(1)}, s32[1,32]{1,0:T(1,128)}, u32[]{:S(2)}) copy-start(s32[1,32]{1,0:T(1,128)} %counts_ref.3) | copy-start | bytes 388
  0.6 31.7 %copy-start.10 = (f32[256]{0:T(256)S(1)}, f32[256]{0:T(256)}, u32[]{:S(2)}) copy-start(f32[256]{0:T(256)} %param.16) | copy-start | bytes 3076
  1.4 2.2 %copy-start = (bf16[1,32,4,128,128]{4,3,2,1,0:T(8,128)(2,1)S(1)}, bf16[1,32,4,128,128]{4,3,2,1,0:T(8,128)(2,1)}, u32[]{:S(2)}) copy-start(bf16[1,32,4,128,128]{4,3,2,1,0:T(8,128)(2,1)} %adj_hbm.3) | copy-start | bytes 12582916
  3.6 0.9 %copy-start.3 = (bf16[4,16384]{1,0:T(4,128)(2,1)S(1)}, bf16[4,16384]{1,0:T(4,128)(2,1)}, u32[]{:S(2)}) copy-start(bf16[4,16384]{1,0:T(4,128)(2,1)} %table_ref.1) | copy-start | bytes 393220
  4.5 0.7 copy-start.7
  5.3 0.7 copy-start.8
  5.9 26.4 %copy-start.4 = (bf16[128,256]{1,0:T(8,128)(2,1)S(1)}, bf16[128,256]{1,0:T(8,128)(2,1)}, u32[]{:S(2)}) copy-start(bf16[128,256]{1,0:T(8,128)(2,1)} %sw_ref.1) | copy-start | bytes 196612
  5.9 26.4 %copy-start.5 = (bf16[128,256]{1,0:T(8,128)(2,1)S(1)}, bf16[128,256]{1,0:T(8,128)(2,1)}, u32[]{:S(2)}) copy-start(bf16[128,256]{1,0:T(8,128)(2,1)} %nw_ref.1) | copy-start | bytes 196612
  5.9 26.4 %copy-start.6 = (bf16[1,128,256]{2,1,0:T(8,128)(2,1)S(1)}, bf16[1,128,256]{2,1,0:T(8,128)(2,1)}, u32[]{:S(2)}) copy-start(bf16[1,128,256]{2,1,0:T(8,128)(2,1)} %cot_ref.1) | copy-start | bytes 196612
  70.6 13.9 %all-to-all-start.3 = ((bf16[32,16,128]{2,1,0:T(8,128)(2,1)}), bf16[32,16,128]{2,1,0:T(8,128)(2,1)S(1)}, u32[]{:S(2)}, u32[]{:S(2)}) async-start(bf16[32,16,128]{2,1,0:T(8,128)(2,1)} %get-tuple-element.13), calls=%async_computation.3 | async-start | bytes 262144 | tf_op jit(solution)/shard_map/all_to_all | solution.py:262
  74.5 2.2 %copy-start.1 = (bf16[1,32,4,128,128]{4,3,2,1,0:T(8,128)(2,1)S(1)}, bf16[1,32,4,128,128]{4,3,2,1,0:T(8,128)(2,1)}, u32[]{:S(2)}) copy-start(bf16[1,32,4,128,128]{4,3,2,1,0:T(8,128)(2,1)} %adj_hbm.3) | copy-start | bytes 12582916
  76.7 0.9 %copy-start.2 = (bf16[32,32,128]{2,1,0:T(8,128)(2,1)S(1)}, bf16[32,32,128]{2,1,0:T(8,128)(2,1)}, u32[]{:S(2)}) copy-start(bf16[32,32,128]{2,1,0:T(8,128)(2,1)} %all_to_all.21.got_ref) | copy-start | bytes 786436
  84.5 0.7 copy-start.11

commit v2 on v1

v2 whole, which is shorter than its diff:
```python
import jax
import jax.numpy as jnp
from jax import lax
from jax.experimental import pallas as pl
from jax.experimental.pallas import tpu as pltpu
from jax.sharding import PartitionSpec as P

F32 = jnp.float32
BF16 = jnp.bfloat16
ADJ_PARTS = 8
LOW = 256
CHUNK = 512
FWD_MIB = 58


def forward_kernel(
    lists_hbm,
    counts_hbm,
    nodes_hbm,
    table_hbm,
    adj_hbm,
    out_ref,
    adj,
    ids_ref,
    counts_ref,
    nodes_ref,
    table_ref,
    rows_f32,
    feats,
    staged,
    sems,
):
    per = adj.shape[0] // ADJ_PARTS
    inputs = [
        pltpu.make_async_copy(table_hbm, table_ref, sems.at[ADJ_PARTS]),
        pltpu.make_async_copy(nodes_hbm, nodes_ref, sems.at[ADJ_PARTS + 1]),
    ]
    lists = [
        pltpu.make_async_copy(lists_hbm, ids_ref, sems.at[ADJ_PARTS + 2]),
        pltpu.make_async_copy(counts_hbm, counts_ref, sems.at[ADJ_PARTS + 3]),
    ]
    copies = [
        pltpu.make_async_copy(
            adj_hbm.at[0, pl.ds(p * per, per)], adj.at[pl.ds(p * per, per)], sems.at[p]
        )
        for p in range(ADJ_PARTS)
    ]
    for copy in inputs + lists + copies:
        copy.start()
    for copy in inputs:
        copy.wait()
    chans = table_ref.shape[0]
    groups = table_ref.shape[1] // LOW
    for q in range(groups):
        rows_f32[q * chans : (q + 1) * chans, :] = table_ref[:, q * LOW : (q + 1) * LOW].astype(F32)
    table_rows = rows_f32[...].astype(BF16)
    node_count = nodes_ref.shape[1]
    for start in range(0, node_count, CHUNK):
        ids = nodes_ref[:, start : start + CHUNK]
        low = ids & (LOW - 1)
        high = ids // LOW
        onehot = jnp.where(lax.broadcasted_iota(jnp.int32, (LOW, CHUNK), 0) == low, 1.0, 0.0)
        spread = jnp.dot(table_rows, onehot.astype(BF16), preferred_element_type=F32)
        group = lax.broadcasted_iota(jnp.int32, spread.shape, 0) // chans
        kept = jnp.where(group == high, spread, 0.0)
        two = jnp.sum(kept.reshape(-1, 8, CHUNK), axis=0)
        both = two + pltpu.roll(two, 4, 0)
        for j in range(CHUNK // 128):
            feats[start // 128 + j] = both[:, j * 128 : (j + 1) * 128]
    for copy in lists:
        copy.wait()
    depth, blocks = ids_ref.shape[1], ids_ref.shape[2]
    side = adj.shape[3]
    upper = lax.broadcasted_iota(jnp.int32, (8, side), 0) < chans
    for b in range(blocks):
        if b % per == 0:
            copies[b // per].wait()
        count = counts_ref[0, b]
        picked = [
            jnp.where(k < count, feats[ids_ref[0, k, b]], 0.0) for k in range(depth)
        ]
        lhs = jnp.concatenate(picked, axis=1).astype(BF16)
        agg = jnp.dot(lhs, adj[b].reshape(depth * side, side), preferred_element_type=F32)
        staged[b] = jnp.where(upper, feats[b], agg)
    out_ref[...] = staged[...].astype(BF16)


def dense_kernel(x_ref, sw_ref, nw_ref, bias_ref, cot_ref, hidden_ref, back_ref, send_ref):
    feats = sw_ref.shape[0]
    hid = sw_ref.shape[1]
    sw = sw_ref[...].astype(F32).reshape(feats // 8, 8, hid)
    nw = nw_ref[...].astype(F32).reshape(feats // 8, 8, hid)
    upper = lax.broadcasted_iota(jnp.int32, sw.shape, 1) < 4
    even = jnp.where(upper, sw, pltpu.roll(nw, 4, 1))
    odd = jnp.where(upper, pltpu.roll(sw, 4, 1), nw)
    weight = jnp.concatenate([even, odd], axis=1).reshape(2 * feats, hid).astype(BF16)
    rows = x_ref.shape[2]
    x = x_ref[...].reshape(2 * feats, rows)
    preact = lax.dot_general(x, weight, (((0,), (0,)), ((), ())), preferred_element_type=F32)
    preact = preact + bias_ref[...]
    sig = jax.nn.sigmoid(preact)
    hidden_ref[0] = (preact * sig).astype(BF16)
    grad_pre = (cot_ref[0].astype(F32) * sig * (1.0 + preact * (1.0 - sig))).astype(BF16)
    grads = jnp.dot(x, grad_pre, preferred_element_type=F32)
    back = lax.dot_general(
        weight, grad_pre, (((1,), (1,)), ((), ())), preferred_element_type=F32
    )
    bias_sum = jnp.sum(grad_pre.astype(F32), axis=0, keepdims=True)
    half = hid // 2
    tail = split_rows(bias_sum[:, :half], bias_sum[:, half:])
    reps = send_ref.shape[0]
    back_ref[...] = back.reshape(back_ref.shape).astype(BF16)
    send_ref[...] = jnp.concatenate(
        [
            grads[:, :half].reshape(reps, -1, half),
            grads[:, half:].reshape(reps, -1, half),
            jnp.broadcast_to(tail[None], (reps, 8, half)),
        ],
        axis=1,
    ).astype(BF16)


def split_rows(first, second):
    place = lax.broadcasted_iota(jnp.int32, (8, first.shape[1]), 0)
    first_hi = first.astype(BF16).astype(F32)
    second_hi = second.astype(BF16).astype(F32)
    out = jnp.where(place == 0, first_hi, 0.0)
    out = jnp.where(place == 1, second_hi, out)
    out = jnp.where(place == 2, first - first_hi, out)
    return jnp.where(place == 3, second - second_hi, out)


def add_up(parts):
    total = jnp.sum(parts, axis=0)
    rows = total.shape[0] - 8
    low = total[rows:]
    return total[:rows], low[0:1] + low[2:3], low[1:2] + low[3:4]


def rep_sum_kernel(got_ref, back_ref, out_ref):
    total, first, second = add_up(got_ref[...].astype(F32))
    whole = jnp.concatenate([total, split_rows(first, second)], axis=0)
    peers = out_ref.shape[0]
    whole = jnp.broadcast_to(whole[None], (peers,) + whole.shape)
    out_ref[...] = jnp.concatenate([back_ref[...].astype(F32), whole], axis=1).astype(BF16)


def feat_sum_kernel(factor, got_ref, out_ref, bias_ref):
    total, first, second = add_up(got_ref[...].astype(F32)[:, 8:, :])
    bias_ref[...] = factor * jnp.concatenate([first, second], axis=1)
    out_ref[...] = jnp.broadcast_to((factor * total).astype(BF16)[None], out_ref.shape)


def assemble_kernel(got_ref, self_ref, neigh_ref):
    side = got_ref.shape[2]
    got = got_ref[...].astype(F32)
    for h in range(2):
        even = got[:, 16 * h : 16 * h + 8]
        odd = got[:, 16 * h + 8 : 16 * h + 16]
        upper = lax.broadcasted_iota(jnp.int32, even.shape, 1) < 4
        first = jnp.where(upper, even, pltpu.roll(odd, 4, 1))
        second = jnp.where(upper, pltpu.roll(even, 4, 1), odd)
        self_ref[:, h * side : (h + 1) * side] = first.reshape(-1, side)
        neigh_ref[:, h * side : (h + 1) * side] = second.reshape(-1, side)


def backward_kernel(ids_ref, counts_ref, got_ref, adj, out_ref, acc):
    acc[...] = jnp.zeros_like(acc)
    depth, blocks = ids_ref.shape[1], ids_ref.shape[2]
    side = adj.shape[3]
    sources = acc.shape[0] - 1
    for b in range(blocks):
        count = counts_ref[0, b]
        lhs = got_ref[b, 0:16, :]
        contrib = lax.dot_general(
            lhs,
            adj[b].reshape(depth * side, side),
            (((1,), (1,)), ((), ())),
            preferred_element_type=F32,
        )
        for k in range(depth):
            place = jnp.where(k < count, ids_ref[0, k, b], sources)
            acc[place] = acc[place] + contrib[0:8, k * side : (k + 1) * side]
    chans = out_ref.shape[1]
    for n in range(sources):
        total = pltpu.roll(acc[n], 4, 0)
        if n < blocks:
            total = total + got_ref[n, 0:16, :].astype(F32)[0:8]
        out_ref[0, :, n * side : (n + 1) * side] = total[0:chans].astype(BF16)


SMEM = pl.BlockSpec(memory_space=pltpu.SMEM)
VMEM = pl.BlockSpec(memory_space=pltpu.VMEM)
HBM = pl.BlockSpec(memory_space=pl.ANY)


def params(mib):
    return pltpu.CompilerParams(vmem_limit_bytes=mib * 1024 * 1024)


def local(
    feature_table,
    node_ids,
    block_ids,
    block_counts,
    adjacency,
    self_weight,
    neigh_weight,
    bias_vector,
    cotangent,
):
    chans = feature_table.shape[0]
    node_count = node_ids.shape[1]
    blocks, depth, side = adjacency.shape[1:4]
    sources = node_count // side
    peers = lax.axis_size("feat")
    reps = lax.axis_size("rep")
    feats, hid = self_weight.shape
    rows = cotangent.shape[1]
    lists = jnp.transpose(block_ids, (0, 2, 1))
    sent = pl.pallas_call(
        forward_kernel,
        out_shape=jax.ShapeDtypeStruct((peers, 8, side), BF16),
        in_specs=[HBM] * 5,
        out_specs=VMEM,
        scratch_shapes=[
            pltpu.VMEM(adjacency.shape[1:], BF16),
            pltpu.SMEM(lists.shape, jnp.int32),
            pltpu.SMEM(block_counts.shape, jnp.int32),
            pltpu.VMEM(node_ids.shape, jnp.int32),
            pltpu.VMEM(feature_table.shape, BF16),
            pltpu.VMEM((feature_table.shape[1] // LOW * chans, LOW), F32),
            pltpu.VMEM((sources, 8, side), F32),
            pltpu.VMEM((peers, 8, side), F32),
            pltpu.SemaphoreType.DMA((ADJ_PARTS + 4,)),
        ],
        compiler_params=params(FWD_MIB),
        name="forward",
    )(lists, block_counts, node_ids, feature_table, adjacency)
    arrived = lax.all_to_all(sent, "feat", split_axis=0, concat_axis=0, tiled=True)
    hidden, back, send = pl.pallas_call(
        dense_kernel,
        out_shape=(
            jax.ShapeDtypeStruct(cotangent.shape, BF16),
            jax.ShapeDtypeStruct((peers, 8, side), BF16),
            jax.ShapeDtypeStruct((reps, 4 * feats // reps + 8, hid // 2), BF16),
        ),
        in_specs=[VMEM] * 5,
        out_specs=(VMEM, VMEM, VMEM),
        compiler_params=params(16),
        name="dense",
    )(arrived, self_weight, neigh_weight, bias_vector.reshape(1, hid), cotangent)
    over_rep = lax.all_to_all(send, "rep", split_axis=0, concat_axis=0, tiled=True)
    rows_sent = send.shape[1]
    merged = pl.pallas_call(
        rep_sum_kernel,
        out_shape=jax.ShapeDtypeStruct((peers, rows_sent + 8, side), BF16),
        in_specs=[VMEM, VMEM],
        out_specs=VMEM,
        compiler_params=params(8),
        name="rep_sum",
    )(over_rep, back)
    got = lax.all_to_all(merged, "feat", split_axis=0, concat_axis=0, tiled=True)
    factor = float(rows * peers * reps) ** (-0.5)
    pieces, bias_grad = pl.pallas_call(
        lambda *refs: feat_sum_kernel(factor, *refs),
        out_shape=(
            jax.ShapeDtypeStruct((reps, rows_sent - 8, side), BF16),
            jax.ShapeDtypeStruct((1, hid), F32),
        ),
        in_specs=[VMEM],
        out_specs=(VMEM, VMEM),
        compiler_params=params(8),
        name="feat_sum",
    )(got)
    whole = lax.all_to_all(pieces, "rep", split_axis=0, concat_axis=0, tiled=True)
    feature_grad = pl.pallas_call(
        backward_kernel,
        out_shape=jax.ShapeDtypeStruct((1, chans, node_count), BF16),
        in_specs=[SMEM, SMEM, VMEM, VMEM],
        out_specs=VMEM,
        scratch_shapes=[pltpu.VMEM((sources + 1, 8, side), F32)],
        compiler_params=params(16),
        cost_estimate=pl.CostEstimate(
            flops=2 * 16 * adjacency.size, bytes_accessed=2 * adjacency.size, transcendentals=0
        ),
        name="spread_back",
    )(lists, block_counts, got, adjacency.reshape(adjacency.shape[1:]))
    self_grad, neigh_grad = pl.pallas_call(
        assemble_kernel,
        out_shape=(
            jax.ShapeDtypeStruct((feats, hid), F32),
            jax.ShapeDtypeStruct((feats, hid), F32),
        ),
        in_specs=[VMEM],
        out_specs=(VMEM, VMEM),
        compiler_params=params(8),
        name="assemble",
    )(whole)
    return hidden, feature_grad, self_grad, neigh_grad, bias_grad.reshape(hid)


def solution(mesh):
    return jax.shard_map(
        local,
        mesh=mesh,
        in_specs=(
            P("feat", None),
            P("rep", None),
            P("rep", None, None),
            P("rep", None),
            P("rep", None, None, None, None),
            P(),
            P(),
            P(),
            P("rep", "feat", None),
        ),
        out_specs=(P("rep", "feat", None), P("rep", "feat", None), P(), P(), P()),
        check_vma=False,
    )
```

time: 87.4 us -> 80.3 us (0.919)
  local copies, waits for them, and re-layouts: 9.07 us -> 2.21 us
  Pallas kernels: 13.7 us -> 9.45 us
  blocking collectives: 56.5 us -> 59.3 us
  waiting for transfers between devices: 2.95 us -> 4.55 us
    unnamed x25 -> x14, local copies, waits for them, and re-layouts: 9.07 us -> 2.21 us
    all_to_all x2, blocking collectives: 34.1 us -> 36.8 us  [the longest x1 18.7 us: local(): lax.all_to_all(send, 'rep', split_axis=0, concat_axis=0, tiled=True)]
    pallas_call x2, Pallas kernels: 3.24 us -> 0.76 us  [the longest x1 0.71 us: local(): pl.pallas_call(lambda *refs: feat_sum_kernel(factor, *refs), out_shape=(j...]
    all_to_all x1, waiting for transfers between devices: 2.95 us -> 4.55 us  [local(): lax.all_to_all(pieces, 'rep', split_axis=0, concat_axis=0, tiled=True)]
    pallas_call x1, Pallas kernels: 3.92 us -> 2.45 us  [local(): pl.pallas_call(backward_kernel, out_shape=jax.ShapeDtypeStruct((1, chans,...]
    pallas_call x1, Pallas kernels: 1.63 us -> 0.72 us  [local(): pl.pallas_call(assemble_kernel, out_shape=(jax.ShapeDtypeStruct((feats, h...]
  transfers between devices with their start and end apart: 1 -> 1, of which waited for: 1 -> 1; matrix products, arithmetic and copies ran while one was open for 0% -> 0% of each run, Pallas kernels for 5% -> 3%
where the time goes in v2:
time: 80.3 us; the launch traced here: 80 us
  blocking collectives  59.3 us (74%)
  Pallas kernels  9.45 us (12%)
  waiting for transfers between devices  4.55 us (6%)
  starting transfers between devices  3.76 us (5%)
  local copies, waits for them, and re-layouts  2.21 us (3%)
    all_to_all x1, blocking collectives, local(): lax.all_to_all(sent, 'feat', split_axis=0, concat_axis=0, tiled=True)  22.5 us
    all_to_all x1, blocking collectives, local(): lax.all_to_all(send, 'rep', split_axis=0, concat_axis=0, tiled=True)  18.7 us
    all_to_all x1, blocking collectives, local(): lax.all_to_all(merged, 'feat', split_axis=0, concat_axis=0, tiled=True)  18.1 us
    pallas_call x1, Pallas kernels, local(): pl.pallas_call(forward_kernel, out_shape=jax.ShapeDtypeStruct((peers, 8,...  4.65 us
    all_to_all x1, waiting for transfers between devices, local(): lax.all_to_all(pieces, 'rep', split_axis=0, concat_axis=0, tiled=True)  4.55 us
    all_to_all x1, starting transfers between devices, local(): lax.all_to_all(pieces, 'rep', split_axis=0, concat_axis=0, tiled=True)  3.76 us
    pallas_call x1, Pallas kernels, local(): pl.pallas_call(backward_kernel, out_shape=jax.ShapeDtypeStruct((1, chans,...  2.45 us
    unnamed x14, local copies, waits for them, and re-layouts  2.21 us
  transfers between devices with their start and end apart: 1, of which 1 were waited for; matrix products, arithmetic and copies ran while one was open for 0% of the time, Pallas kernels for 3%

profile of v2, /device:TPU:1, one launch (start us, length us, event | category | flops | bytes accessed | tf_op | source)
XLA Modules:
  0.0 80.0 jit_solution(6131339527636031415)
XLA Ops:
  0.6 0.0 copy-start.5
  0.6 0.0 copy-start.4
  0.7 0.0 copy-start.3
  0.7 0.0 copy-start.6
  0.7 0.0 copy-start.2
  0.7 0.0 copy-start.1
  0.7 4.7 %forward.1 = bf16[32,8,128]{2,1,0:T(8,128)(2,1)} custom-call(s32[1,4,32]{2,1,0:T(4,128)} %bitcast.5, s32[1,32]{1,0:T(1,128)} %counts_ref.1, s32[1,6144]{1,0:T(1,128)} %nodes_hbm.1, bf16[4,16384]{1,0:T(4,128)(2,1)} %table_hbm.1, bf16[1,32,4,128,128]{4,3,2,1,0:T(8,128)(2,1)} %adj_hbm.1), custom_call_target="tpu_custom_call" | custom-call | tf_op jit(solution)/shard_map/forward/pallas_call | solution.py:221
  5.4 22.5 %all_to_all.20.x_ref = bf16[32,8,128]{2,1,0:T(8,128)(2,1)S(1)} all-to-all(bf16[32,8,128]{2,1,0:T(8,128)(2,1)} %forward.1), channel_id=1, replica_groups=mesh['feat'=32,'rep'=16] {'feat'}, dimensions={0} | all-to-all | bytes 131072 | tf_op jit(solution)/shard_map/all_to_all | solution.py:240
  27.9 0.0 copy-done.3
  27.9 0.0 copy-done.6
  27.9 0.0 copy-done.2
  27.9 0.0 copy-done.1
  27.9 0.9 %dense.1 = (bf16[1,128,256]{2,1,0:T(8,128)(2,1)}, bf16[32,8,128]{2,1,0:T(8,128)(2,1)S(1)}, bf16[16,40,128]{2,1,0:T(8,128)(2,1)S(1)}) custom-call(bf16[32,8,128]{2,1,0:T(8,128)(2,1)S(1)} %all_to_all.20.x_ref, bf16[128,256]{1,0:T(8,128)(2,1)S(1)} %copy-done.1, bf16[128,256]{1,0:T(8,128)(2,1)S(1)} %copy-done.2, f32[1,256]{1,0:T(1,128)S(1)} %bitcast.7, ...), custom_call_target="tpu_custom_call" | custom-call | tf_op jit(solution)/shard_map/dense/pallas_call | solution.py:241
  28.8 18.7 %all_to_all.21.got_ref = bf16[16,40,128]{2,1,0:T(8,128)(2,1)S(1)} all-to-all(bf16[16,40,128]{2,1,0:T(8,128)(2,1)S(1)} %get-tuple-element.13), channel_id=1, replica_groups=mesh['feat'=32,'rep'=16] {'rep'}, dimensions={0} | all-to-all | bytes 327680 | tf_op jit(solution)/shard_map/all_to_all | solution.py:253
  47.4 0.1 rep_sum.1
  47.5 18.1 %all_to_all.22.got_ref.refs_0_ = bf16[32,48,128]{2,1,0:T(8,128)(2,1)S(1)} all-to-all(bf16[32,48,128]{2,1,0:T(8,128)(2,1)S(1)} %rep_sum.1), channel_id=1, replica_groups=mesh['feat'=32,'rep'=16] {'feat'}, dimensions={0} | all-to-all | bytes 786432 | tf_op jit(solution)/shard_map/all_to_all | solution.py:263
  65.6 0.7 feat_sum.1
  66.3 3.8 %all-to-all-start.3 = ((bf16[16,32,128]{2,1,0:T(8,128)(2,1)}), bf16[16,32,128]{2,1,0:T(8,128)(2,1)S(1)}, u32[]{:S(2)}, u32[]{:S(2)}) async-start(bf16[16,32,128]{2,1,0:T(8,128)(2,1)} %get-tuple-element.15), calls=%async_computation.3 | async-start | bytes 262144 | tf_op jit(solution)/shard_map/all_to_all | solution.py:276
  70.1 0.0 copy-done.5
  70.1 0.0 copy-done.4
  70.1 0.0 copy-start
  70.1 2.2 %copy-done = bf16[1,32,4,128,128]{4,3,2,1,0:T(8,128)(2,1)S(1)} copy-done((bf16[1,32,4,128,128]{4,3,2,1,0:T(8,128)(2,1)S(1)}, bf16[1,32,4,128,128]{4,3,2,1,0:T(8,128)(2,1)}, u32[]{:S(2)}) %copy-start) | copy-done | bytes 4194328
  72.3 2.5 %spread_back.1 = bf16[1,4,6144]{2,1,0:T(4,128)(2,1)} custom-call(s32[1,4,32]{2,1,0:T(4,128)S(1)} %bitcast.6, s32[1,32]{1,0:T(1,128)S(1)} %copy-done.5, bf16[32,48,128]{2,1,0:T(8,128)(2,1)S(1)} %all_to_all.22.got_ref.refs_0_, bf16[32,4,128,128]{3,2,1,0:T(8,128)(2,1)S(1)} %bitcast.4), custom_call_target="tpu_custom_call" | custom-call | flops 67108864 | bytes 4194304 | tf_op jit(solution)/shard_map/spread_back/pallas_call | solution.py:277
  74.7 4.6 %all-to-all-done.3.got_ref = bf16[16,32,128]{2,1,0:T(8,128)(2,1)S(1)} async-done(((bf16[16,32,128]{2,1,0:T(8,128)(2,1)}), bf16[16,32,128]{2,1,0:T(8,128)(2,1)S(1)}, u32[]{:S(2)}, u32[]{:S(2)}) %all-to-all-start.3) | async-done | bytes 131104 | tf_op jit(solution)/shard_map/all_to_all | solution.py:276
  79.3 0.7 assemble.1
Async XLA Ops:
  0.6 69.4 %copy-start.5 = (s32[1,32]{1,0:T(1,128)S(1)}, s32[1,32]{1,0:T(1,128)}, u32[]{:S(2)}) copy-start(s32[1,32]{1,0:T(1,128)} %counts_ref.1) | copy-start | bytes 388
  0.6 69.4 %copy-start.4 = (s32[1,32,4]{1,2,0:T(4,128)S(1)}, s32[1,32,4]{1,2,0:T(4,128)}, u32[]{:S(2)}) copy-start(s32[1,32,4]{1,2,0:T(4,128)} %param.11) | copy-start | bytes 1540
  0.7 27.2 %copy-start.3 = (bf16[1,128,256]{2,1,0:T(8,128)(2,1)S(1)}, bf16[1,128,256]{2,1,0:T(8,128)(2,1)}, u32[]{:S(2)}) copy-start(bf16[1,128,256]{2,1,0:T(8,128)(2,1)} %cot_ref.1) | copy-start | bytes 196612
  0.7 27.2 %copy-start.6 = (f32[256]{0:T(256)S(1)}, f32[256]{0:T(256)}, u32[]{:S(2)}) copy-start(f32[256]{0:T(256)} %param.16) | copy-start | bytes 3076
  0.7 27.2 %copy-start.2 = (bf16[128,256]{1,0:T(8,128)(2,1)S(1)}, bf16[128,256]{1,0:T(8,128)(2,1)}, u32[]{:S(2)}) copy-start(bf16[128,256]{1,0:T(8,128)(2,1)} %nw_ref.1) | copy-start | bytes 196612
  0.7 27.2 %copy-start.1 = (bf16[128,256]{1,0:T(8,128)(2,1)S(1)}, bf16[128,256]{1,0:T(8,128)(2,1)}, u32[]{:S(2)}) copy-start(bf16[128,256]{1,0:T(8,128)(2,1)} %sw_ref.1) | copy-start | bytes 196612
  66.3 13.0 %all-to-all-start.3 = ((bf16[16,32,128]{2,1,0:T(8,128)(2,1)}), bf16[16,32,128]{2,1,0:T(8,128)(2,1)S(1)}, u32[]{:S(2)}, u32[]{:S(2)}) async-start(bf16[16,32,128]{2,1,0:T(8,128)(2,1)} %get-tuple-element.15), calls=%async_computation.3 | async-start | bytes 262144 | tf_op jit(solution)/shard_map/all_to_all | solution.py:276
  70.1 2.2 %copy-start = (bf16[1,32,4,128,128]{4,3,2,1,0:T(8,128)(2,1)S(1)}, bf16[1,32,4,128,128]{4,3,2,1,0:T(8,128)(2,1)}, u32[]{:S(2)}) copy-start(bf16[1,32,4,128,128]{4,3,2,1,0:T(8,128)(2,1)} %adj_hbm.1) | copy-start | bytes 12582916

commit v3 on v2

--- a/solution.py
+++ b/solution.py
@@ -85,7 +85,7 @@
     out_ref[...] = staged[...].astype(BF16)
 
 
-def dense_kernel(x_ref, sw_ref, nw_ref, bias_ref, cot_ref, hidden_ref, back_ref, send_ref):
+def dense_kernel(x_ref, sw_ref, nw_ref, bias_ref, cot_ref, hidden_ref, send_ref):
     feats = sw_ref.shape[0]
     hid = sw_ref.shape[1]
     sw = sw_ref[...].astype(F32).reshape(feats // 8, 8, hid)
@@ -108,13 +108,13 @@
     bias_sum = jnp.sum(grad_pre.astype(F32), axis=0, keepdims=True)
     half = hid // 2
     tail = split_rows(bias_sum[:, :half], bias_sum[:, half:])
-    reps = send_ref.shape[0]
-    back_ref[...] = back.reshape(back_ref.shape).astype(BF16)
+    peers = send_ref.shape[0]
     send_ref[...] = jnp.concatenate(
         [
-            grads[:, :half].reshape(reps, -1, half),
-            grads[:, half:].reshape(reps, -1, half),
-            jnp.broadcast_to(tail[None], (reps, 8, half)),
+            back.reshape(peers, 8, rows),
+            grads[:, :half].reshape(peers, 8, half),
+            grads[:, half:].reshape(peers, 8, half),
+            jnp.broadcast_to(tail[None], (peers, 8, half)),
         ],
         axis=1,
     ).astype(BF16)
@@ -137,26 +137,24 @@
     return total[:rows], low[0:1] + low[2:3], low[1:2] + low[3:4]
 
 
-def rep_sum_kernel(got_ref, back_ref, out_ref):
+def feat_sum_kernel(got_ref, out_ref):
+    total, first, second = add_up(got_ref[...].astype(F32)[:, 8:, :])
+    whole = jnp.concatenate([total, split_rows(first, second)], axis=0).astype(BF16)
+    out_ref[...] = jnp.broadcast_to(whole[None], out_ref.shape)
+
+
+def rep_sum_kernel(factor, got_ref, out_ref, bias_ref):
     total, first, second = add_up(got_ref[...].astype(F32))
-    whole = jnp.concatenate([total, split_rows(first, second)], axis=0)
-    peers = out_ref.shape[0]
-    whole = jnp.broadcast_to(whole[None], (peers,) + whole.shape)
-    out_ref[...] = jnp.concatenate([back_ref[...].astype(F32), whole], axis=1).astype(BF16)
-
-
-def feat_sum_kernel(factor, got_ref, out_ref, bias_ref):
-    total, first, second = add_up(got_ref[...].astype(F32)[:, 8:, :])
     bias_ref[...] = factor * jnp.concatenate([first, second], axis=1)
     out_ref[...] = jnp.broadcast_to((factor * total).astype(BF16)[None], out_ref.shape)
 
 
 def assemble_kernel(got_ref, self_ref, neigh_ref):
-    side = got_ref.shape[2]
-    got = got_ref[...].astype(F32)
+    peers, _, side = got_ref.shape
+    got = got_ref[...].astype(F32).reshape(peers // 2, 32, side)
     for h in range(2):
-        even = got[:, 16 * h : 16 * h + 8]
-        odd = got[:, 16 * h + 8 : 16 * h + 16]
+        even = got[:, 8 * h : 8 * h + 8]
+        odd = got[:, 16 + 8 * h : 24 + 8 * h]
         upper = lax.broadcasted_iota(jnp.int32, even.shape, 1) < 4
         first = jnp.where(upper, even, pltpu.roll(odd, 4, 1))
         second = jnp.where(upper, pltpu.roll(even, 4, 1), odd)
@@ -238,42 +236,40 @@
         name="forward",
     )(lists, block_counts, node_ids, feature_table, adjacency)
     arrived = lax.all_to_all(sent, "feat", split_axis=0, concat_axis=0, tiled=True)
-    hidden, back, send = pl.pallas_call(
+    hidden, send = pl.pallas_call(
         dense_kernel,
         out_shape=(
             jax.ShapeDtypeStruct(cotangent.shape, BF16),
-            jax.ShapeDtypeStruct((peers, 8, side), BF16),
-            jax.ShapeDtypeStruct((reps, 4 * feats // reps + 8, hid // 2), BF16),
+            jax.ShapeDtypeStruct((peers, 32, side), BF16),
         ),
         in_specs=[VMEM] * 5,
-        out_specs=(VMEM, VMEM, VMEM),
+        out_specs=(VMEM, VMEM),
         compiler_params=params(16),
         name="dense",
     )(arrived, self_weight, neigh_weight, bias_vector.reshape(1, hid), cotangent)
-    over_rep = lax.all_to_all(send, "rep", split_axis=0, concat_axis=0, tiled=True)
-    rows_sent = send.shape[1]
-    merged = pl.pallas_call(
-        rep_sum_kernel,
-        out_shape=jax.ShapeDtypeStruct((peers, rows_sent + 8, side), BF16),
-        in_specs=[VMEM, VMEM],
+    got = lax.all_to_all(send, "feat", split_axis=0, concat_axis=0, tiled=True)
+    partial = pl.pallas_call(
+        feat_sum_kernel,
+        out_shape=jax.ShapeDtypeStruct((reps, 24, side), BF16),
+        in_specs=[VMEM],
         out_specs=VMEM,
         compiler_params=params(8),
-        name="rep_sum",
-    )(over_rep, back)
-    got = lax.all_to_all(merged, "feat", split_axis=0, concat_axis=0, tiled=True)
+        name="feat_sum",
+    )(got)
+    over_rep = lax.all_to_all(partial, "rep", split_axis=0, concat_axis=0, tiled=True)
     factor = float(rows * peers * reps) ** (-0.5)
     pieces, bias_grad = pl.pallas_call(
-        lambda *refs: feat_sum_kernel(factor, *refs),
+        lambda *refs: rep_sum_kernel(factor, *refs),
         out_shape=(
-            jax.ShapeDtypeStruct((reps, rows_sent - 8, side), BF16),
+            jax.ShapeDtypeStruct((peers, 16, side), BF16),
             jax.ShapeDtypeStruct((1, hid), F32),
         ),
         in_specs=[VMEM],
         out_specs=(VMEM, VMEM),
         compiler_params=params(8),
-        name="feat_sum",
-    )(got)
-    whole = lax.all_to_all(pieces, "rep", split_axis=0, concat_axis=0, tiled=True)
+        name="rep_sum",
+    )(over_rep)
+    whole = lax.all_to_all(pieces, "feat", split_axis=0, concat_axis=0, tiled=True)
     feature_grad = pl.pallas_call(
         backward_kernel,
         out_shape=jax.ShapeDtypeStruct((1, chans, node_count), BF16),

time: 80.3 us -> 77 us (0.959)
  blocking collectives: 59.3 us -> 55.2 us
    all_to_all x2, blocking collectives: 36.8 us -> 32.7 us  [the longest x1 19.2 us: local(): lax.all_to_all(partial, 'rep', split_axis=0, concat_axis=0, tiled=True)]
where the time goes in v3:
time: 77 us; the launch traced here: 76.7 us
  blocking collectives  55.2 us (72%)
  Pallas kernels  9.43 us (12%)
  waiting for transfers between devices  5.22 us (7%)
  starting transfers between devices  3.86 us (5%)
  local copies, waits for them, and re-layouts  2.21 us (3%)
    all_to_all x1, blocking collectives, local(): lax.all_to_all(sent, 'feat', split_axis=0, concat_axis=0, tiled=True)  22.5 us
    all_to_all x1, blocking collectives, local(): lax.all_to_all(partial, 'rep', split_axis=0, concat_axis=0, tiled=True)  19.2 us
    all_to_all x1, blocking collectives, local(): got = lax.all_to_all(send, 'feat', split_axis=0, concat_axis=0, tiled=True)  13.5 us
    all_to_all x1, waiting for transfers between devices, local(): lax.all_to_all(pieces, 'feat', split_axis=0, concat_axis=0, tiled=True)  5.22 us
    pallas_call x1, Pallas kernels, local(): pl.pallas_call(forward_kernel, out_shape=jax.ShapeDtypeStruct((peers, 8,...  4.65 us
    all_to_all x1, starting transfers between devices, local(): lax.all_to_all(pieces, 'feat', split_axis=0, concat_axis=0, tiled=True)  3.86 us
    pallas_call x1, Pallas kernels, local(): pl.pallas_call(backward_kernel, out_shape=jax.ShapeDtypeStruct((1, chans,...  2.46 us
    unnamed x14, local copies, waits for them, and re-layouts  2.21 us
  transfers between devices with their start and end apart: 1, of which 1 were waited for; matrix products, arithmetic and copies ran while one was open for 0% of the time, Pallas kernels for 3%

profile of v3, /device:TPU:1, one launch (start us, length us, event | category | flops | bytes accessed | tf_op | source)
XLA Modules:
  0.0 76.7 jit_solution(12737155607106613103)
XLA Ops:
  0.6 0.0 copy-start.5
  0.6 0.0 copy-start.4
  0.7 0.0 copy-start.3
  0.7 0.0 copy-start.6
  0.7 0.0 copy-start.2
  0.7 0.0 copy-start.1
  0.7 4.7 %forward.1 = bf16[32,8,128]{2,1,0:T(8,128)(2,1)} custom-call(s32[1,4,32]{2,1,0:T(4,128)} %bitcast.5, s32[1,32]{1,0:T(1,128)} %counts_ref.1, s32[1,6144]{1,0:T(1,128)} %nodes_hbm.1, bf16[4,16384]{1,0:T(4,128)(2,1)} %table_hbm.1, bf16[1,32,4,128,128]{4,3,2,1,0:T(8,128)(2,1)} %adj_hbm.1), custom_call_target="tpu_custom_call" | custom-call | tf_op jit(solution)/shard_map/forward/pallas_call | solution.py:219
  5.4 22.5 %all_to_all.20.x_ref = bf16[32,8,128]{2,1,0:T(8,128)(2,1)S(1)} all-to-all(bf16[32,8,128]{2,1,0:T(8,128)(2,1)} %forward.1), channel_id=1, replica_groups=mesh['feat'=32,'rep'=16] {'feat'}, dimensions={0} | all-to-all | bytes 131072 | tf_op jit(solution)/shard_map/all_to_all | solution.py:238
  27.9 0.0 copy-done.3
  27.9 0.0 copy-done.6
  27.9 0.0 copy-done.2
  27.9 0.0 copy-done.1
  27.9 0.9 %dense.1 = (bf16[1,128,256]{2,1,0:T(8,128)(2,1)}, bf16[32,32,128]{2,1,0:T(8,128)(2,1)S(1)}) custom-call(bf16[32,8,128]{2,1,0:T(8,128)(2,1)S(1)} %all_to_all.20.x_ref, bf16[128,256]{1,0:T(8,128)(2,1)S(1)} %copy-done.1, bf16[128,256]{1,0:T(8,128)(2,1)S(1)} %copy-done.2, f32[1,256]{1,0:T(1,128)S(1)} %bitcast.7, bf16[1,128,256]{2,1,0:T(8,128)(2,1)S(1)} %copy-done.3), custom_call_target="tpu_custom_call" | custom-call | tf_op jit(solution)/shard_map/dense/pallas_call | solution.py:239
  28.8 13.5 %all_to_all.21.got_ref = bf16[32,32,128]{2,1,0:T(8,128)(2,1)S(1)} all-to-all(bf16[32,32,128]{2,1,0:T(8,128)(2,1)S(1)} %get-tuple-element.12), channel_id=1, replica_groups=mesh['feat'=32,'rep'=16] {'feat'}, dimensions={0} | all-to-all | bytes 524288 | tf_op jit(solution)/shard_map/all_to_all | solution.py:250
  42.3 19.2 %all_to_all.22.refs_0_ = bf16[16,24,128]{2,1,0:T(8,128)(2,1)S(1)} all-to-all(bf16[16,24,128]{2,1,0:T(8,128)(2,1)S(1)} %feat_sum.1), channel_id=1, replica_groups=mesh['feat'=32,'rep'=16] {'rep'}, dimensions={0} | all-to-all | bytes 196608 | tf_op jit(solution)/shard_map/all_to_all | solution.py:259
  61.5 0.7 rep_sum.1
  62.2 3.9 %all-to-all-start.3 = ((bf16[32,16,128]{2,1,0:T(8,128)(2,1)}), bf16[32,16,128]{2,1,0:T(8,128)(2,1)S(1)}, u32[]{:S(2)}, u32[]{:S(2)}) async-start(bf16[32,16,128]{2,1,0:T(8,128)(2,1)} %get-tuple-element.13), calls=%async_computation.3 | async-start | bytes 262144 | tf_op jit(solution)/shard_map/all_to_all | solution.py:272
  66.0 0.0 copy-done.5
  66.1 0.0 copy-done.4
  66.1 0.0 copy-start
  66.1 2.2 %copy-done = bf16[1,32,4,128,128]{4,3,2,1,0:T(8,128)(2,1)S(1)} copy-done((bf16[1,32,4,128,128]{4,3,2,1,0:T(8,128)(2,1)S(1)}, bf16[1,32,4,128,128]{4,3,2,1,0:T(8,128)(2,1)}, u32[]{:S(2)}) %copy-start) | copy-done | bytes 4194328
  68.3 2.5 %spread_back.1 = bf16[1,4,6144]{2,1,0:T(4,128)(2,1)} custom-call(s32[1,4,32]{2,1,0:T(4,128)S(1)} %bitcast.6, s32[1,32]{1,0:T(1,128)S(1)} %copy-done.5, bf16[32,32,128]{2,1,0:T(8,128)(2,1)S(1)} %all_to_all.21.got_ref, bf16[32,4,128,128]{3,2,1,0:T(8,128)(2,1)S(1)} %bitcast.4), custom_call_target="tpu_custom_call" | custom-call | flops 67108864 | bytes 4194304 | tf_op jit(solution)/shard_map/spread_back/pallas_call | solution.py:273
  70.7 5.2 %all-to-all-done.3.got_ref = bf16[32,16,128]{2,1,0:T(8,128)(2,1)S(1)} async-done(((bf16[32,16,128]{2,1,0:T(8,128)(2,1)}), bf16[32,16,128]{2,1,0:T(8,128)(2,1)S(1)}, u32[]{:S(2)}, u32[]{:S(2)}) %all-to-all-start.3) | async-done | bytes 131104 | tf_op jit(solution)/shard_map/all_to_all | solution.py:272
  75.9 0.7 assemble.1
  (1 shorter events, 0.0 us)
Async XLA Ops:
  0.6 65.4 %copy-start.5 = (s32[1,32]{1,0:T(1,128)S(1)}, s32[1,32]{1,0:T(1,128)}, u32[]{:S(2)}) copy-start(s32[1,32]{1,0:T(1,128)} %counts_ref.1) | copy-start | bytes 388
  0.6 65.4 %copy-start.4 = (s32[1,32,4]{1,2,0:T(4,128)S(1)}, s32[1,32,4]{1,2,0:T(4,128)}, u32[]{:S(2)}) copy-start(s32[1,32,4]{1,2,0:T(4,128)} %param.11) | copy-start | bytes 1540
  0.7 27.2 %copy-start.3 = (bf16[1,128,256]{2,1,0:T(8,128)(2,1)S(1)}, bf16[1,128,256]{2,1,0:T(8,128)(2,1)}, u32[]{:S(2)}) copy-start(bf16[1,128,256]{2,1,0:T(8,128)(2,1)} %cot_ref.1) | copy-start | bytes 196612
  0.7 27.2 %copy-start.6 = (f32[256]{0:T(256)S(1)}, f32[256]{0:T(256)}, u32[]{:S(2)}) copy-start(f32[256]{0:T(256)} %param.16) | copy-start | bytes 3076
  0.7 27.2 %copy-start.2 = (bf16[128,256]{1,0:T(8,128)(2,1)S(1)}, bf16[128,256]{1,0:T(8,128)(2,1)}, u32[]{:S(2)}) copy-start(bf16[128,256]{1,0:T(8,128)(2,1)} %nw_ref.1) | copy-start | bytes 196612
  0.7 27.2 %copy-start.1 = (bf16[128,256]{1,0:T(8,128)(2,1)S(1)}, bf16[128,256]{1,0:T(8,128)(2,1)}, u32[]{:S(2)}) copy-start(bf16[128,256]{1,0:T(8,128)(2,1)} %sw_ref.1) | copy-start | bytes 196612
  62.2 13.8 %all-to-all-start.3 = ((bf16[32,16,128]{2,1,0:T(8,128)(2,1)}), bf16[32,16,128]{2,1,0:T(8,128)(2,1)S(1)}, u32[]{:S(2)}, u32[]{:S(2)}) async-start(bf16[32,16,128]{2,1,0:T(8,128)(2,1)} %get-tuple-element.13), calls=%async_computation.3 | async-start | bytes 262144 | tf_op jit(solution)/shard_map/all_to_all | solution.py:272
  66.1 2.2 %copy-start = (bf16[1,32,4,128,128]{4,3,2,1,0:T(8,128)(2,1)S(1)}, bf16[1,32,4,128,128]{4,3,2,1,0:T(8,128)(2,1)}, u32[]{:S(2)}) copy-start(bf16[1,32,4,128,128]{4,3,2,1,0:T(8,128)(2,1)} %adj_hbm.1) | copy-start | bytes 12582916

commit v4 on v3

--- a/solution.py
+++ b/solution.py
@@ -10,7 +10,16 @@
 ADJ_PARTS = 8
 LOW = 256
 CHUNK = 512
-FWD_MIB = 58
+
+
+def adj_copies(adj_hbm, adj, sems):
+    per = adj.shape[0] // ADJ_PARTS
+    return per, [
+        pltpu.make_async_copy(
+            adj_hbm.at[0, pl.ds(p * per, per)], adj.at[pl.ds(p * per, per)], sems.at[p]
+        )
+        for p in range(ADJ_PARTS)
+    ]
 
 
 def forward_kernel(
@@ -30,7 +39,7 @@
     staged,
     sems,
 ):
-    per = adj.shape[0] // ADJ_PARTS
+    per, copies = adj_copies(adj_hbm, adj, sems)
     inputs = [
         pltpu.make_async_copy(table_hbm, table_ref, sems.at[ADJ_PARTS]),
         pltpu.make_async_copy(nodes_hbm, nodes_ref, sems.at[ADJ_PARTS + 1]),
@@ -38,12 +47,6 @@
     lists = [
         pltpu.make_async_copy(lists_hbm, ids_ref, sems.at[ADJ_PARTS + 2]),
         pltpu.make_async_copy(counts_hbm, counts_ref, sems.at[ADJ_PARTS + 3]),
-    ]
-    copies = [
-        pltpu.make_async_copy(
-            adj_hbm.at[0, pl.ds(p * per, per)], adj.at[pl.ds(p * per, per)], sems.at[p]
-        )
-        for p in range(ADJ_PARTS)
     ]
     for copy in inputs + lists + copies:
         copy.start()
@@ -55,12 +58,15 @@
         rows_f32[q * chans : (q + 1) * chans, :] = table_ref[:, q * LOW : (q + 1) * LOW].astype(F32)
     table_rows = rows_f32[...].astype(BF16)
     node_count = nodes_ref.shape[1]
+    column = lax.broadcasted_iota(jnp.int32, (LOW, CHUNK), 0).astype(F32).astype(BF16)
+    one = jnp.ones((LOW, CHUNK), BF16)
+    zero = jnp.zeros((LOW, CHUNK), BF16)
     for start in range(0, node_count, CHUNK):
         ids = nodes_ref[:, start : start + CHUNK]
         low = ids & (LOW - 1)
         high = ids // LOW
-        onehot = jnp.where(lax.broadcasted_iota(jnp.int32, (LOW, CHUNK), 0) == low, 1.0, 0.0)
-        spread = jnp.dot(table_rows, onehot.astype(BF16), preferred_element_type=F32)
+        onehot = jnp.where(column == low.astype(F32).astype(BF16), one, zero)
+        spread = jnp.dot(table_rows, onehot, preferred_element_type=F32)
         group = lax.broadcasted_iota(jnp.int32, spread.shape, 0) // chans
         kept = jnp.where(group == high, spread, 0.0)
         two = jnp.sum(kept.reshape(-1, 8, CHUNK), axis=0)
@@ -162,12 +168,20 @@
         neigh_ref[:, h * side : (h + 1) * side] = second.reshape(-1, side)
 
 
-def backward_kernel(ids_ref, counts_ref, got_ref, adj, out_ref, acc):
+def backward_kernel(
+    ids_ref, counts_ref, got_ref, hid_ref, adj_hbm, out_ref, hidden_ref, adj, acc, sems
+):
+    per, copies = adj_copies(adj_hbm, adj, sems)
+    for copy in copies:
+        copy.start()
+    hidden_ref[...] = hid_ref[...]
     acc[...] = jnp.zeros_like(acc)
     depth, blocks = ids_ref.shape[1], ids_ref.shape[2]
     side = adj.shape[3]
     sources = acc.shape[0] - 1
     for b in range(blocks):
+        if b % per == 0:
+            copies[b // per].wait()
         count = counts_ref[0, b]
         lhs = got_ref[b, 0:16, :]
         contrib = lax.dot_general(
@@ -190,6 +204,10 @@
 SMEM = pl.BlockSpec(memory_space=pltpu.SMEM)
 VMEM = pl.BlockSpec(memory_space=pltpu.VMEM)
 HBM = pl.BlockSpec(memory_space=pl.ANY)
+
+
+def in_hbm(array):
+    return pltpu.with_memory_space_constraint(array, pltpu.HBM)
 
 
 def params(mib):
@@ -232,11 +250,11 @@
             pltpu.VMEM((peers, 8, side), F32),
             pltpu.SemaphoreType.DMA((ADJ_PARTS + 4,)),
         ],
-        compiler_params=params(FWD_MIB),
+        compiler_params=params(24),
         name="forward",
-    )(lists, block_counts, node_ids, feature_table, adjacency)
+    )(*[in_hbm(v) for v in (lists, block_counts, node_ids, feature_table, adjacency)])
     arrived = lax.all_to_all(sent, "feat", split_axis=0, concat_axis=0, tiled=True)
-    hidden, send = pl.pallas_call(
+    hid_vmem, send = pl.pallas_call(
         dense_kernel,
         out_shape=(
             jax.ShapeDtypeStruct(cotangent.shape, BF16),
@@ -270,18 +288,25 @@
         name="rep_sum",
     )(over_rep)
     whole = lax.all_to_all(pieces, "feat", split_axis=0, concat_axis=0, tiled=True)
-    feature_grad = pl.pallas_call(
+    feature_grad, hidden = pl.pallas_call(
         backward_kernel,
-        out_shape=jax.ShapeDtypeStruct((1, chans, node_count), BF16),
-        in_specs=[SMEM, SMEM, VMEM, VMEM],
-        out_specs=VMEM,
-        scratch_shapes=[pltpu.VMEM((sources + 1, 8, side), F32)],
-        compiler_params=params(16),
+        out_shape=(
+            jax.ShapeDtypeStruct((1, chans, node_count), BF16),
+            jax.ShapeDtypeStruct(cotangent.shape, BF16),
+        ),
+        in_specs=[SMEM, SMEM, VMEM, VMEM, HBM],
+        out_specs=(VMEM, VMEM),
+        scratch_shapes=[
+            pltpu.VMEM(adjacency.shape[1:], BF16),
+            pltpu.VMEM((sources + 1, 8, side), F32),
+            pltpu.SemaphoreType.DMA((ADJ_PARTS,)),
+        ],
+        compiler_params=params(24),
         cost_estimate=pl.CostEstimate(
             flops=2 * 16 * adjacency.size, bytes_accessed=2 * adjacency.size, transcendentals=0
         ),
         name="spread_back",
-    )(lists, block_counts, got, adjacency.reshape(adjacency.shape[1:]))
+    )(lists, block_counts, got, hid_vmem, in_hbm(adjacency))
     self_grad, neigh_grad = pl.pallas_call(
         assemble_kernel,
         out_shape=(

time: 77 us -> 75.3 us (0.978)
  local copies, waits for them, and re-layouts: 2.21 us -> 0.03 us
    unnamed x14 -> x12, local copies, waits for them, and re-layouts: 2.21 us -> 0.03 us
    pallas_call x1, Pallas kernels: 2.46 us -> 4.41 us  [local(): pl.pallas_call(backward_kernel, out_shape=(jax.ShapeDtypeStruct((1, chans...]
    pallas_call x1, Pallas kernels: 4.65 us -> 3.66 us  [local(): pl.pallas_call(forward_kernel, out_shape=jax.ShapeDtypeStruct((peers, 8,...]
  transfers between devices with their start and end apart: 1 -> 1, of which waited for: 1 -> 1; matrix products, arithmetic and copies ran while one was open for 0% -> 0% of each run, Pallas kernels for 3% -> 6%
where the time goes in v4:
time: 75.3 us; the launch traced here: 75.1 us
  blocking collectives  55 us (73%)
  Pallas kernels  9.98 us (13%)
  waiting for transfers between devices  5.45 us (7%)
  starting transfers between devices  3.86 us (5%)
    all_to_all x1, blocking collectives, local(): lax.all_to_all(sent, 'feat', split_axis=0, concat_axis=0, tiled=True)  22.3 us
    all_to_all x1, blocking collectives, local(): lax.all_to_all(partial, 'rep', split_axis=0, concat_axis=0, tiled=True)  19.2 us
    all_to_all x1, blocking collectives, local(): got = lax.all_to_all(send, 'feat', split_axis=0, concat_axis=0, tiled=True)  13.5 us
    all_to_all x1, waiting for transfers between devices, local(): lax.all_to_all(pieces, 'feat', split_axis=0, concat_axis=0, tiled=True)  5.45 us
    pallas_call x1, Pallas kernels, local(): pl.pallas_call(backward_kernel, out_shape=(jax.ShapeDtypeStruct((1, chans...  4.41 us
    all_to_all x1, starting transfers between devices, local(): lax.all_to_all(pieces, 'feat', split_axis=0, concat_axis=0, tiled=True)  3.86 us
    pallas_call x1, Pallas kernels, local(): pl.pallas_call(forward_kernel, out_shape=jax.ShapeDtypeStruct((peers, 8,...  3.66 us
  transfers between devices with their start and end apart: 1, of which 1 were waited for; matrix products, arithmetic and copies ran while one was open for 0% of the time, Pallas kernels for 6%

profile of v4, /device:TPU:1, one launch (start us, length us, event | category | flops | bytes accessed | tf_op | source)
XLA Modules:
  0.0 75.1 jit_solution(7666412566043607628)
XLA Ops:
  0.6 0.0 copy-start.4
  0.6 0.0 copy-start.3
  0.7 0.0 copy-start.2
  0.7 0.0 copy-start.5
  0.7 0.0 copy-start.1
  0.7 0.0 copy-start
  0.7 3.7 %forward.1 = bf16[32,8,128]{2,1,0:T(8,128)(2,1)S(1)} custom-call(s32[1,4,32]{2,1,0:T(4,128)} %bitcast.3, s32[1,32]{1,0:T(1,128)} %counts_ref.1, s32[1,6144]{1,0:T(1,128)} %nodes_hbm.1, bf16[4,16384]{1,0:T(4,128)(2,1)} %table_hbm.1, bf16[1,32,4,128,128]{4,3,2,1,0:T(8,128)(2,1)} %adj_hbm.3), custom_call_target="tpu_custom_call" | custom-call | tf_op jit(solution)/shard_map/forward/pallas_call | solution.py:237
  4.4 22.3 %all_to_all.20.x_ref = bf16[32,8,128]{2,1,0:T(8,128)(2,1)S(1)} all-to-all(bf16[32,8,128]{2,1,0:T(8,128)(2,1)S(1)} %forward.1), channel_id=1, replica_groups=mesh['feat'=32,'rep'=16] {'feat'}, dimensions={0} | all-to-all | bytes 131072 | tf_op jit(solution)/shard_map/all_to_all | solution.py:256
  26.7 0.0 copy-done.2
  26.7 0.0 copy-done.5
  26.7 0.0 copy-done.1
  26.7 0.0 copy-done
  26.7 0.5 dense.1
  27.2 13.5 %all_to_all.21.got_ref = bf16[32,32,128]{2,1,0:T(8,128)(2,1)S(1)} all-to-all(bf16[32,32,128]{2,1,0:T(8,128)(2,1)S(1)} %get-tuple-element.13), channel_id=1, replica_groups=mesh['feat'=32,'rep'=16] {'feat'}, dimensions={0} | all-to-all | bytes 524288 | tf_op jit(solution)/shard_map/all_to_all | solution.py:268
  40.7 19.2 %all_to_all.22.refs_0_ = bf16[16,24,128]{2,1,0:T(8,128)(2,1)S(1)} all-to-all(bf16[16,24,128]{2,1,0:T(8,128)(2,1)S(1)} %feat_sum.1), channel_id=1, replica_groups=mesh['feat'=32,'rep'=16] {'rep'}, dimensions={0} | all-to-all | bytes 196608 | tf_op jit(solution)/shard_map/all_to_all | solution.py:277
  59.9 0.7 rep_sum.1
  60.6 3.9 %all-to-all-start.3 = ((bf16[32,16,128]{2,1,0:T(8,128)(2,1)}), bf16[32,16,128]{2,1,0:T(8,128)(2,1)S(1)}, u32[]{:S(2)}, u32[]{:S(2)}) async-start(bf16[32,16,128]{2,1,0:T(8,128)(2,1)} %get-tuple-element.17), calls=%async_computation.3 | async-start | bytes 262144 | tf_op jit(solution)/shard_map/all_to_all | solution.py:290
  64.5 0.0 copy-done.4
  64.5 0.0 copy-done.3
  64.5 4.4 %spread_back.1 = (bf16[1,4,6144]{2,1,0:T(4,128)(2,1)}, bf16[1,128,256]{2,1,0:T(8,128)(2,1)}) custom-call(s32[1,4,32]{2,1,0:T(4,128)S(1)} %bitcast.4, s32[1,32]{1,0:T(1,128)S(1)} %copy-done.4, bf16[32,32,128]{2,1,0:T(8,128)(2,1)S(1)} %all_to_all.21.got_ref, bf16[1,128,256]{2,1,0:T(8,128)(2,1)S(1)} %get-tuple-element.14.hid_ref, ...), custom_call_target="tpu_custom_call" | custom-call | flops 67108864 | bytes 4194304 | tf_op jit(solution)/shard_map/spread_back/pallas_call | solution.py:291
  68.9 5.4 %all-to-all-done.3.got_ref = bf16[32,16,128]{2,1,0:T(8,128)(2,1)S(1)} async-done(((bf16[32,16,128]{2,1,0:T(8,128)(2,1)}), bf16[32,16,128]{2,1,0:T(8,128)(2,1)S(1)}, u32[]{:S(2)}, u32[]{:S(2)}) %all-to-all-start.3) | async-done | bytes 131104 | tf_op jit(solution)/shard_map/all_to_all | solution.py:290
  74.3 0.7 assemble.1
  (1 shorter events, 0.0 us)
Async XLA Ops:
  0.6 63.8 %copy-start.4 = (s32[1,32]{1,0:T(1,128)S(1)}, s32[1,32]{1,0:T(1,128)}, u32[]{:S(2)}) copy-start(s32[1,32]{1,0:T(1,128)} %counts_ref.1) | copy-start | bytes 388
  0.6 63.8 %copy-start.3 = (s32[1,32,4]{1,2,0:T(4,128)S(1)}, s32[1,32,4]{1,2,0:T(4,128)}, u32[]{:S(2)}) copy-start(s32[1,32,4]{1,2,0:T(4,128)} %param.11) | copy-start | bytes 1540
  0.7 26.0 %copy-start.2 = (bf16[1,128,256]{2,1,0:T(8,128)(2,1)S(1)}, bf16[1,128,256]{2,1,0:T(8,128)(2,1)}, u32[]{:S(2)}) copy-start(bf16[1,128,256]{2,1,0:T(8,128)(2,1)} %cot_ref.1) | copy-start | bytes 196612
  0.7 26.0 %copy-start.5 = (f32[256]{0:T(256)S(1)}, f32[256]{0:T(256)}, u32[]{:S(2)}) copy-start(f32[256]{0:T(256)} %param.16) | copy-start | bytes 3076
  0.7 26.0 %copy-start.1 = (bf16[128,256]{1,0:T(8,128)(2,1)S(1)}, bf16[128,256]{1,0:T(8,128)(2,1)}, u32[]{:S(2)}) copy-start(bf16[128,256]{1,0:T(8,128)(2,1)} %nw_ref.1) | copy-start | bytes 196612
  0.7 26.0 %copy-start = (bf16[128,256]{1,0:T(8,128)(2,1)S(1)}, bf16[128,256]{1,0:T(8,128)(2,1)}, u32[]{:S(2)}) copy-start(bf16[128,256]{1,0:T(8,128)(2,1)} %sw_ref.1) | copy-start | bytes 196612
  60.6 13.8 %all-to-all-start.3 = ((bf16[32,16,128]{2,1,0:T(8,128)(2,1)}), bf16[32,16,128]{2,1,0:T(8,128)(2,1)S(1)}, u32[]{:S(2)}, u32[]{:S(2)}) async-start(bf16[32,16,128]{2,1,0:T(8,128)(2,1)} %get-tuple-element.17), calls=%async_computation.3 | async-start | bytes 262144 | tf_op jit(solution)/shard_map/all_to_all | solution.py:290

commit v5 on v4

--- a/solution.py
+++ b/solution.py
@@ -7,7 +7,7 @@
 
 F32 = jnp.float32
 BF16 = jnp.bfloat16
-ADJ_PARTS = 8
+ADJ_PARTS = 2
 LOW = 256
 CHUNK = 512
 
@@ -115,19 +115,15 @@
     half = hid // 2
     tail = split_rows(bias_sum[:, :half], bias_sum[:, half:])
     peers = send_ref.shape[0]
-    send_ref[...] = jnp.concatenate(
-        [
-            back.reshape(peers, 8, rows),
-            grads[:, :half].reshape(peers, 8, half),
-            grads[:, half:].reshape(peers, 8, half),
-            jnp.broadcast_to(tail[None], (peers, 8, half)),
-        ],
-        axis=1,
-    ).astype(BF16)
+    values = [back.reshape(peers, 8, rows)]
+    values += [grads[:, at : at + half].reshape(peers, 8, half) for at in (0, half)]
+    parts = [v[:, at : at + 4] for v in values for at in (0, 4)]
+    parts.append(jnp.broadcast_to(tail[None], (peers, 4, half)))
+    send_ref[...] = jnp.concatenate(parts, axis=2).astype(BF16)
 
 
 def split_rows(first, second):
-    place = lax.broadcasted_iota(jnp.int32, (8, first.shape[1]), 0)
+    place = lax.broadcasted_iota(jnp.int32, (4, first.shape[1]), 0)
     first_hi = first.astype(BF16).astype(F32)
     second_hi = second.astype(BF16).astype(F32)
     out = jnp.where(place == 0, first_hi, 0.0)
@@ -138,14 +134,14 @@
 
 def add_up(parts):
     total = jnp.sum(parts, axis=0)
-    rows = total.shape[0] - 8
-    low = total[rows:]
-    return total[:rows], low[0:1] + low[2:3], low[1:2] + low[3:4]
+    cols = total.shape[1] - 128
+    low = total[:, cols:]
+    return total[:, :cols], low[0:1] + low[2:3], low[1:2] + low[3:4]
 
 
 def feat_sum_kernel(got_ref, out_ref):
-    total, first, second = add_up(got_ref[...].astype(F32)[:, 8:, :])
-    whole = jnp.concatenate([total, split_rows(first, second)], axis=0).astype(BF16)
+    total, first, second = add_up(got_ref[...].astype(F32)[:, :, 256:])
+    whole = jnp.concatenate([total, split_rows(first, second)], axis=1).astype(BF16)
     out_ref[...] = jnp.broadcast_to(whole[None], out_ref.shape)
 
 
@@ -156,16 +152,12 @@
 
 
 def assemble_kernel(got_ref, self_ref, neigh_ref):
-    peers, _, side = got_ref.shape
-    got = got_ref[...].astype(F32).reshape(peers // 2, 32, side)
+    got = got_ref[...].astype(F32)
+    side = got.shape[2] // 4
     for h in range(2):
-        even = got[:, 8 * h : 8 * h + 8]
-        odd = got[:, 16 + 8 * h : 24 + 8 * h]
-        upper = lax.broadcasted_iota(jnp.int32, even.shape, 1) < 4
-        first = jnp.where(upper, even, pltpu.roll(odd, 4, 1))
-        second = jnp.where(upper, pltpu.roll(even, 4, 1), odd)
-        self_ref[:, h * side : (h + 1) * side] = first.reshape(-1, side)
-        neigh_ref[:, h * side : (h + 1) * side] = second.reshape(-1, side)
+        for j, out_ref in enumerate((self_ref, neigh_ref)):
+            at = (2 * h + j) * side
+            out_ref[:, h * side : (h + 1) * side] = got[:, :, at : at + side].reshape(-1, side)
 
 
 def backward_kernel(
@@ -183,7 +175,7 @@
         if b % per == 0:
             copies[b // per].wait()
         count = counts_ref[0, b]
-        lhs = got_ref[b, 0:16, :]
+        lhs = got_ref[b, :, side : 2 * side]
         contrib = lax.dot_general(
             lhs,
             adj[b].reshape(depth * side, side),
@@ -192,13 +184,12 @@
         )
         for k in range(depth):
             place = jnp.where(k < count, ids_ref[0, k, b], sources)
-            acc[place] = acc[place] + contrib[0:8, k * side : (k + 1) * side]
-    chans = out_ref.shape[1]
+            acc[place] = acc[place] + contrib[:, k * side : (k + 1) * side]
     for n in range(sources):
-        total = pltpu.roll(acc[n], 4, 0)
+        total = acc[n]
         if n < blocks:
-            total = total + got_ref[n, 0:16, :].astype(F32)[0:8]
-        out_ref[0, :, n * side : (n + 1) * side] = total[0:chans].astype(BF16)
+            total = total + got_ref[n, :, 0:side].astype(F32)
+        out_ref[0, :, n * side : (n + 1) * side] = total.astype(BF16)
 
 
 SMEM = pl.BlockSpec(memory_space=pltpu.SMEM)
@@ -258,7 +249,7 @@
         dense_kernel,
         out_shape=(
             jax.ShapeDtypeStruct(cotangent.shape, BF16),
-            jax.ShapeDtypeStruct((peers, 32, side), BF16),
+            jax.ShapeDtypeStruct((peers, chans, 7 * side), BF16),
         ),
         in_specs=[VMEM] * 5,
         out_specs=(VMEM, VMEM),
@@ -268,7 +259,7 @@
     got = lax.all_to_all(send, "feat", split_axis=0, concat_axis=0, tiled=True)
     partial = pl.pallas_call(
         feat_sum_kernel,
-        out_shape=jax.ShapeDtypeStruct((reps, 24, side), BF16),
+        out_shape=jax.ShapeDtypeStruct((reps, chans, 5 * side), BF16),
         in_specs=[VMEM],
         out_specs=VMEM,
         compiler_params=params(8),
@@ -279,7 +270,7 @@
     pieces, bias_grad = pl.pallas_call(
         lambda *refs: rep_sum_kernel(factor, *refs),
         out_shape=(
-            jax.ShapeDtypeStruct((peers, 16, side), BF16),
+            jax.ShapeDtypeStruct((peers, chans, 4 * side), BF16),
             jax.ShapeDtypeStruct((1, hid), F32),
         ),
         in_specs=[VMEM],
@@ -298,7 +289,7 @@
         out_specs=(VMEM, VMEM),
         scratch_shapes=[
             pltpu.VMEM(adjacency.shape[1:], BF16),
-            pltpu.VMEM((sources + 1, 8, side), F32),
+            pltpu.VMEM((sources + 1, chans, side), F32),
             pltpu.SemaphoreType.DMA((ADJ_PARTS,)),
         ],
         compiler_params=params(24),

time: 75.3 us -> 73.6 us (0.977)
  blocking collectives: 55 us -> 54 us
  Pallas kernels: 9.98 us -> 9.05 us
    pallas_call x1, Pallas kernels: 3.66 us -> 2.89 us  [local(): pl.pallas_call(forward_kernel, out_shape=jax.ShapeDtypeStruct((peers, 8,...]
where the time goes in v5:
time: 73.6 us; the launch traced here: 73.4 us
  blocking collectives  54 us (73%)
  Pallas kernels  9.05 us (12%)
  waiting for transfers between devices  5.64 us (8%)
  starting transfers between devices  3.86 us (5%)
  between operations  0.74 us (1%)
    all_to_all x1, blocking collectives, local(): lax.all_to_all(sent, 'feat', split_axis=0, concat_axis=0, tiled=True)  22.3 us
    all_to_all x1, blocking collectives, local(): lax.all_to_all(partial, 'rep', split_axis=0, concat_axis=0, tiled=True)  18.4 us
    all_to_all x1, blocking collectives, local(): got = lax.all_to_all(send, 'feat', split_axis=0, concat_axis=0, tiled=True)  13.3 us
    all_to_all x1, waiting for transfers between devices, local(): lax.all_to_all(pieces, 'feat', split_axis=0, concat_axis=0, tiled=True)  5.64 us
    pallas_call x1, Pallas kernels, local(): pl.pallas_call(backward_kernel, out_shape=(jax.ShapeDtypeStruct((1, chans...  4.19 us
    all_to_all x1, starting transfers between devices, local(): lax.all_to_all(pieces, 'feat', split_axis=0, concat_axis=0, tiled=True)  3.86 us
    pallas_call x1, Pallas kernels, local(): pl.pallas_call(forward_kernel, out_shape=jax.ShapeDtypeStruct((peers, 8,...  2.89 us
  transfers between devices with their start and end apart: 1, of which 1 were waited for; matrix products, arithmetic and copies ran while one was open for 0% of the time, Pallas kernels for 6%

profile of v5, /device:TPU:1, one launch (start us, length us, event | category | flops | bytes accessed | tf_op | source)
XLA Modules:
  0.0 73.4 jit_solution(7513473825272889413)
XLA Ops:
  0.6 0.0 copy-start.4
  0.6 0.0 copy-start.3
  0.7 0.0 copy-start.2
  0.7 0.0 copy-start.5
  0.7 0.0 copy-start.1
  0.7 0.0 copy-start
  0.7 2.9 %forward.1 = bf16[32,8,128]{2,1,0:T(8,128)(2,1)S(1)} custom-call(s32[1,4,32]{2,1,0:T(4,128)} %bitcast.3, s32[1,32]{1,0:T(1,128)} %counts_ref.1, s32[1,6144]{1,0:T(1,128)} %nodes_hbm.1, bf16[4,16384]{1,0:T(4,128)(2,1)} %table_hbm.1, bf16[1,32,4,128,128]{4,3,2,1,0:T(8,128)(2,1)} %adj_hbm.3), custom_call_target="tpu_custom_call" | custom-call | tf_op jit(solution)/shard_map/forward/pallas_call | solution.py:228
  3.6 22.3 %all_to_all.20.x_ref = bf16[32,8,128]{2,1,0:T(8,128)(2,1)S(1)} all-to-all(bf16[32,8,128]{2,1,0:T(8,128)(2,1)S(1)} %forward.1), channel_id=1, replica_groups=mesh['feat'=32,'rep'=16] {'feat'}, dimensions={0} | all-to-all | bytes 131072 | tf_op jit(solution)/shard_map/all_to_all | solution.py:247
  25.9 0.0 copy-done.2
  25.9 0.0 copy-done.5
  25.9 0.0 copy-done.1
  25.9 0.0 copy-done
  25.9 0.5 dense.1
  26.4 13.3 %all_to_all.21.got_ref = bf16[32,4,896]{2,1,0:T(4,128)(2,1)S(1)} all-to-all(bf16[32,4,896]{2,1,0:T(4,128)(2,1)S(1)} %get-tuple-element.13), channel_id=1, replica_groups=mesh['feat'=32,'rep'=16] {'feat'}, dimensions={0} | all-to-all | bytes 458752 | tf_op jit(solution)/shard_map/all_to_all | solution.py:259
  39.7 0.1 feat_sum.1
  39.8 18.4 %all_to_all.22.refs_0_ = bf16[16,4,640]{2,1,0:T(4,128)(2,1)S(1)} all-to-all(bf16[16,4,640]{2,1,0:T(4,128)(2,1)S(1)} %feat_sum.1), channel_id=1, replica_groups=mesh['feat'=32,'rep'=16] {'rep'}, dimensions={0} | all-to-all | bytes 163840 | tf_op jit(solution)/shard_map/all_to_all | solution.py:268
  58.2 0.7 rep_sum.1
  58.9 3.9 %all-to-all-start.3 = ((bf16[32,4,512]{2,1,0:T(4,128)(2,1)}), bf16[32,4,512]{2,1,0:T(4,128)(2,1)S(1)}, u32[]{:S(2)}, u32[]{:S(2)}) async-start(bf16[32,4,512]{2,1,0:T(4,128)(2,1)} %get-tuple-element.17), calls=%async_computation.3 | async-start | bytes 262144 | tf_op jit(solution)/shard_map/all_to_all | solution.py:281
  62.8 0.0 copy-done.4
  62.8 0.0 copy-done.3
  62.8 4.2 %spread_back.1 = (bf16[1,4,6144]{2,1,0:T(4,128)(2,1)}, bf16[1,128,256]{2,1,0:T(8,128)(2,1)}) custom-call(s32[1,4,32]{2,1,0:T(4,128)S(1)} %bitcast.4, s32[1,32]{1,0:T(1,128)S(1)} %copy-done.4, bf16[32,4,896]{2,1,0:T(4,128)(2,1)S(1)} %all_to_all.21.got_ref, bf16[1,128,256]{2,1,0:T(8,128)(2,1)S(1)} %get-tuple-element.14.hid_ref, ...), custom_call_target="tpu_custom_call" | custom-call | flops 67108864 | bytes 4194304 | tf_op jit(solution)/shard_map/spread_back/pallas_call | solution.py:282
  67.0 5.6 %all-to-all-done.3.got_ref = bf16[32,4,512]{2,1,0:T(4,128)(2,1)S(1)} async-done(((bf16[32,4,512]{2,1,0:T(4,128)(2,1)}), bf16[32,4,512]{2,1,0:T(4,128)(2,1)S(1)}, u32[]{:S(2)}, u32[]{:S(2)}) %all-to-all-start.3) | async-done | bytes 131104 | tf_op jit(solution)/shard_map/all_to_all | solution.py:281
  72.6 0.7 assemble.1
Async XLA Ops:
  0.6 62.2 %copy-start.4 = (s32[1,32]{1,0:T(1,128)S(1)}, s32[1,32]{1,0:T(1,128)}, u32[]{:S(2)}) copy-start(s32[1,32]{1,0:T(1,128)} %counts_ref.1) | copy-start | bytes 388
  0.6 62.2 %copy-start.3 = (s32[1,32,4]{1,2,0:T(4,128)S(1)}, s32[1,32,4]{1,2,0:T(4,128)}, u32[]{:S(2)}) copy-start(s32[1,32,4]{1,2,0:T(4,128)} %param.11) | copy-start | bytes 1540
  0.7 25.3 %copy-start.2 = (bf16[1,128,256]{2,1,0:T(8,128)(2,1)S(1)}, bf16[1,128,256]{2,1,0:T(8,128)(2,1)}, u32[]{:S(2)}) copy-start(bf16[1,128,256]{2,1,0:T(8,128)(2,1)} %cot_ref.1) | copy-start | bytes 196612
  0.7 25.3 %copy-start.5 = (f32[256]{0:T(256)S(1)}, f32[256]{0:T(256)}, u32[]{:S(2)}) copy-start(f32[256]{0:T(256)} %param.16) | copy-start | bytes 3076
  0.7 25.3 %copy-start.1 = (bf16[128,256]{1,0:T(8,128)(2,1)S(1)}, bf16[128,256]{1,0:T(8,128)(2,1)}, u32[]{:S(2)}) copy-start(bf16[128,256]{1,0:T(8,128)(2,1)} %nw_ref.1) | copy-start | bytes 196612
  0.7 25.3 %copy-start = (bf16[128,256]{1,0:T(8,128)(2,1)S(1)}, bf16[128,256]{1,0:T(8,128)(2,1)}, u32[]{:S(2)}) copy-start(bf16[128,256]{1,0:T(8,128)(2,1)} %sw_ref.1) | copy-start | bytes 196612
  58.9 13.7 %all-to-all-start.3 = ((bf16[32,4,512]{2,1,0:T(4,128)(2,1)}), bf16[32,4,512]{2,1,0:T(4,128)(2,1)S(1)}, u32[]{:S(2)}, u32[]{:S(2)}) async-start(bf16[32,4,512]{2,1,0:T(4,128)(2,1)} %get-tuple-element.17), calls=%async_computation.3 | async-start | bytes 262144 | tf_op jit(solution)/shard_map/all_to_all | solution.py:281

commit v6 on v5

--- a/solution.py
+++ b/solution.py
@@ -7,19 +7,9 @@
 
 F32 = jnp.float32
 BF16 = jnp.bfloat16
-ADJ_PARTS = 2
+HELD = 16
 LOW = 256
 CHUNK = 512
-
-
-def adj_copies(adj_hbm, adj, sems):
-    per = adj.shape[0] // ADJ_PARTS
-    return per, [
-        pltpu.make_async_copy(
-            adj_hbm.at[0, pl.ds(p * per, per)], adj.at[pl.ds(p * per, per)], sems.at[p]
-        )
-        for p in range(ADJ_PARTS)
-    ]
 
 
 def forward_kernel(
@@ -29,7 +19,8 @@
     table_hbm,
     adj_hbm,
     out_ref,
-    adj,
+    held,
+    rest,
     ids_ref,
     counts_ref,
     nodes_ref,
@@ -39,14 +30,18 @@
     staged,
     sems,
 ):
-    per, copies = adj_copies(adj_hbm, adj, sems)
+    blocks, _, side, _ = adj_hbm.shape[1:]
+    copies = [
+        pltpu.make_async_copy(adj_hbm.at[0, pl.ds(0, HELD)], held, sems.at[0]),
+        pltpu.make_async_copy(adj_hbm.at[0, pl.ds(HELD, blocks - HELD)], rest, sems.at[1]),
+    ]
     inputs = [
-        pltpu.make_async_copy(table_hbm, table_ref, sems.at[ADJ_PARTS]),
-        pltpu.make_async_copy(nodes_hbm, nodes_ref, sems.at[ADJ_PARTS + 1]),
+        pltpu.make_async_copy(table_hbm, table_ref, sems.at[2]),
+        pltpu.make_async_copy(nodes_hbm, nodes_ref, sems.at[3]),
     ]
     lists = [
-        pltpu.make_async_copy(lists_hbm, ids_ref, sems.at[ADJ_PARTS + 2]),
-        pltpu.make_async_copy(counts_hbm, counts_ref, sems.at[ADJ_PARTS + 3]),
+        pltpu.make_async_copy(lists_hbm, ids_ref, sems.at[4]),
+        pltpu.make_async_copy(counts_hbm, counts_ref, sems.at[5]),
     ]
     for copy in inputs + lists + copies:
         copy.start()
@@ -75,18 +70,18 @@
             feats[start // 128 + j] = both[:, j * 128 : (j + 1) * 128]
     for copy in lists:
         copy.wait()
-    depth, blocks = ids_ref.shape[1], ids_ref.shape[2]
-    side = adj.shape[3]
+    depth = ids_ref.shape[1]
     upper = lax.broadcasted_iota(jnp.int32, (8, side), 0) < chans
     for b in range(blocks):
-        if b % per == 0:
-            copies[b // per].wait()
+        if b in (0, HELD):
+            copies[b // HELD].wait()
+        adj = held[b] if b < HELD else rest[b - HELD]
         count = counts_ref[0, b]
         picked = [
             jnp.where(k < count, feats[ids_ref[0, k, b]], 0.0) for k in range(depth)
         ]
         lhs = jnp.concatenate(picked, axis=1).astype(BF16)
-        agg = jnp.dot(lhs, adj[b].reshape(depth * side, side), preferred_element_type=F32)
+        agg = jnp.dot(lhs, adj.reshape(depth * side, side), preferred_element_type=F32)
         staged[b] = jnp.where(upper, feats[b], agg)
     out_ref[...] = staged[...].astype(BF16)
 
@@ -145,40 +140,51 @@
     out_ref[...] = jnp.broadcast_to(whole[None], out_ref.shape)
 
 
-def rep_sum_kernel(factor, got_ref, out_ref, bias_ref):
+def rep_sum_kernel(factor, got_ref, after_ref, out_ref, bias_ref):
     total, first, second = add_up(got_ref[...].astype(F32))
     bias_ref[...] = factor * jnp.concatenate([first, second], axis=1)
     out_ref[...] = jnp.broadcast_to((factor * total).astype(BF16)[None], out_ref.shape)
 
 
-def assemble_kernel(got_ref, self_ref, neigh_ref):
-    got = got_ref[...].astype(F32)
-    side = got.shape[2] // 4
-    for h in range(2):
-        for j, out_ref in enumerate((self_ref, neigh_ref)):
+def assemble_kernel(
+    got_ref, bias_ref, self_hbm, neigh_hbm, bias_hbm, self_ref, neigh_ref, sems
+):
+    side = got_ref.shape[2] // 4
+    copies = [pltpu.make_async_copy(bias_ref, bias_hbm, sems.at[2])]
+    copies[0].start()
+    for j, (out_ref, out_hbm) in enumerate(((self_ref, self_hbm), (neigh_ref, neigh_hbm))):
+        for h in range(2):
             at = (2 * h + j) * side
-            out_ref[:, h * side : (h + 1) * side] = got[:, :, at : at + side].reshape(-1, side)
+            got = got_ref[:, :, at : at + side].astype(F32)
+            out_ref[:, h * side : (h + 1) * side] = got.reshape(-1, side)
+        copy = pltpu.make_async_copy(out_ref, out_hbm, sems.at[j])
+        copy.start()
+        copies.append(copy)
+    for copy in copies:
+        copy.wait()
 
 
 def backward_kernel(
-    ids_ref, counts_ref, got_ref, hid_ref, adj_hbm, out_ref, hidden_ref, adj, acc, sems
+    ids_ref, counts_ref, got_ref, hid_ref, held, adj_hbm, out_ref, hidden_ref, rest, acc, sems
 ):
-    per, copies = adj_copies(adj_hbm, adj, sems)
-    for copy in copies:
-        copy.start()
+    blocks, _, side, _ = adj_hbm.shape[1:]
+    copy = pltpu.make_async_copy(
+        adj_hbm.at[0, pl.ds(HELD, blocks - HELD)], rest, sems.at[0]
+    )
+    copy.start()
     hidden_ref[...] = hid_ref[...]
     acc[...] = jnp.zeros_like(acc)
-    depth, blocks = ids_ref.shape[1], ids_ref.shape[2]
-    side = adj.shape[3]
+    depth = ids_ref.shape[1]
     sources = acc.shape[0] - 1
     for b in range(blocks):
-        if b % per == 0:
-            copies[b // per].wait()
+        if b == HELD:
+            copy.wait()
+        adj = held[b] if b < HELD else rest[b - HELD]
         count = counts_ref[0, b]
         lhs = got_ref[b, :, side : 2 * side]
         contrib = lax.dot_general(
             lhs,
-            adj[b].reshape(depth * side, side),
+            adj.reshape(depth * side, side),
             (((1,), (1,)), ((), ())),
             preferred_element_type=F32,
         )
@@ -225,13 +231,18 @@
     feats, hid = self_weight.shape
     rows = cotangent.shape[1]
     lists = jnp.transpose(block_ids, (0, 2, 1))
-    sent = pl.pallas_call(
+    held_shape = (HELD, depth, side, side)
+    rest_shape = (blocks - HELD, depth, side, side)
+    sent, held = pl.pallas_call(
         forward_kernel,
-        out_shape=jax.ShapeDtypeStruct((peers, 8, side), BF16),
+        out_shape=(
+            jax.ShapeDtypeStruct((peers, 8, side), BF16),
+            jax.ShapeDtypeStruct(held_shape, BF16),
+        ),
         in_specs=[HBM] * 5,
-        out_specs=VMEM,
+        out_specs=(VMEM, VMEM),
         scratch_shapes=[
-            pltpu.VMEM(adjacency.shape[1:], BF16),
+            pltpu.VMEM(rest_shape, BF16),
             pltpu.SMEM(lists.shape, jnp.int32),
             pltpu.SMEM(block_counts.shape, jnp.int32),
             pltpu.VMEM(node_ids.shape, jnp.int32),
@@ -239,7 +250,7 @@
             pltpu.VMEM((feature_table.shape[1] // LOW * chans, LOW), F32),
             pltpu.VMEM((sources, 8, side), F32),
             pltpu.VMEM((peers, 8, side), F32),
-            pltpu.SemaphoreType.DMA((ADJ_PARTS + 4,)),
+            pltpu.SemaphoreType.DMA((6,)),
         ],
         compiler_params=params(24),
         name="forward",
@@ -267,48 +278,54 @@
     )(got)
     over_rep = lax.all_to_all(partial, "rep", split_axis=0, concat_axis=0, tiled=True)
     factor = float(rows * peers * reps) ** (-0.5)
-    pieces, bias_grad = pl.pallas_call(
-        lambda *refs: rep_sum_kernel(factor, *refs),
-        out_shape=(
-            jax.ShapeDtypeStruct((peers, chans, 4 * side), BF16),
-            jax.ShapeDtypeStruct((1, hid), F32),
-        ),
-        in_specs=[VMEM],
-        out_specs=(VMEM, VMEM),
-        compiler_params=params(8),
-        name="rep_sum",
-    )(over_rep)
-    whole = lax.all_to_all(pieces, "feat", split_axis=0, concat_axis=0, tiled=True)
     feature_grad, hidden = pl.pallas_call(
         backward_kernel,
         out_shape=(
             jax.ShapeDtypeStruct((1, chans, node_count), BF16),
             jax.ShapeDtypeStruct(cotangent.shape, BF16),
         ),
-        in_specs=[SMEM, SMEM, VMEM, VMEM, HBM],
+        in_specs=[SMEM, SMEM, VMEM, VMEM, VMEM, HBM],
         out_specs=(VMEM, VMEM),
         scratch_shapes=[
-            pltpu.VMEM(adjacency.shape[1:], BF16),
+            pltpu.VMEM(rest_shape, BF16),
             pltpu.VMEM((sources + 1, chans, side), F32),
-            pltpu.SemaphoreType.DMA((ADJ_PARTS,)),
+            pltpu.SemaphoreType.DMA((1,)),
         ],
         compiler_params=params(24),
         cost_estimate=pl.CostEstimate(
             flops=2 * 16 * adjacency.size, bytes_accessed=2 * adjacency.size, transcendentals=0
         ),
         name="spread_back",
-    )(lists, block_counts, got, hid_vmem, in_hbm(adjacency))
-    self_grad, neigh_grad = pl.pallas_call(
+    )(lists, block_counts, got, hid_vmem, held, in_hbm(adjacency))
+    pieces, bias_sum = pl.pallas_call(
+        lambda *refs: rep_sum_kernel(factor, *refs),
+        out_shape=(
+            jax.ShapeDtypeStruct((peers, chans, 4 * side), BF16),
+            jax.ShapeDtypeStruct((1, hid), F32),
+        ),
+        in_specs=[VMEM, HBM],
+        out_specs=(VMEM, VMEM),
+        compiler_params=params(8),
+        name="rep_sum",
+    )(over_rep, in_hbm(hidden))
+    whole = lax.all_to_all(pieces, "feat", split_axis=0, concat_axis=0, tiled=True)
+    self_grad, neigh_grad, bias_grad = pl.pallas_call(
         assemble_kernel,
         out_shape=(
             jax.ShapeDtypeStruct((feats, hid), F32),
             jax.ShapeDtypeStruct((feats, hid), F32),
-        ),
-        in_specs=[VMEM],
-        out_specs=(VMEM, VMEM),
+            jax.ShapeDtypeStruct((1, hid), F32),
+        ),
+        in_specs=[VMEM, VMEM],
+        out_specs=(HBM, HBM, HBM),
+        scratch_shapes=[
+            pltpu.VMEM((feats, hid), F32),
+            pltpu.VMEM((feats, hid), F32),
+            pltpu.SemaphoreType.DMA((3,)),
+        ],
         compiler_params=params(8),
         name="assemble",
-    )(whole)
+    )(whole, bias_sum)
     return hidden, feature_grad, self_grad, neigh_grad, bias_grad.reshape(hid)
 
 

time: 73.6 us -> 73.2 us (level)
  starting transfers between devices: 3.86 us -> 10.5 us
  blocking collectives: 54 us -> 48.7 us
  waiting for transfers between devices: 5.64 us -> 4.15 us
    all_to_all x1, starting transfers between devices: 3.86 us -> 10.5 us  [local(): lax.all_to_all(partial, 'rep', split_axis=0, concat_axis=0, tiled=True)]
    all_to_all x1, blocking collectives: 18.4 us -> 13.1 us  [local(): lax.all_to_all(pieces, 'feat', split_axis=0, concat_axis=0, tiled=True)]
    all_to_all x1, waiting for transfers between devices: 5.64 us -> 4.15 us  [local(): lax.all_to_all(partial, 'rep', split_axis=0, concat_axis=0, tiled=True)]
  transfers between devices with their start and end apart: 1 -> 1, of which waited for: 1 -> 1; matrix products, arithmetic and copies ran while one was open for 0% -> 0% of each run, Pallas kernels for 6% -> 5%
where the time goes in v6:
time: 73.2 us; the launch traced here: 72.9 us
  blocking collectives  48.7 us (67%)
  starting transfers between devices  10.5 us (14%)
  Pallas kernels  8.83 us (12%)
  waiting for transfers between devices  4.15 us (6%)
    all_to_all x1, blocking collectives, local(): lax.all_to_all(sent, 'feat', split_axis=0, concat_axis=0, tiled=True)  22.3 us
    all_to_all x1, blocking collectives, local(): got = lax.all_to_all(send, 'feat', split_axis=0, concat_axis=0, tiled=True)  13.3 us
    all_to_all x1, blocking collectives, local(): lax.all_to_all(pieces, 'feat', split_axis=0, concat_axis=0, tiled=True)  13.1 us
    all_to_all x1, starting transfers between devices, local(): lax.all_to_all(partial, 'rep', split_axis=0, concat_axis=0, tiled=True)  10.5 us
    all_to_all x1, waiting for transfers between devices, local(): lax.all_to_all(partial, 'rep', split_axis=0, concat_axis=0, tiled=True)  4.15 us
    pallas_call x1, Pallas kernels, local(): pl.pallas_call(backward_kernel, out_shape=(jax.ShapeDtypeStruct((1, chans...  3.97 us
    pallas_call x1, Pallas kernels, local(): pl.pallas_call(forward_kernel, out_shape=(jax.ShapeDtypeStruct((peers, 8,...  2.88 us
  transfers between devices with their start and end apart: 1, of which 1 were waited for; matrix products, arithmetic and copies ran while one was open for 0% of the time, Pallas kernels for 5%

profile of v6, /device:TPU:1, one launch (start us, length us, event | category | flops | bytes accessed | tf_op | source)
XLA Modules:
  0.0 72.9 jit_solution(4326365436891597086)
XLA Ops:
  0.6 0.0 copy-start.4
  0.6 0.0 copy-start.3
  0.7 0.0 copy-start.2
  0.7 0.0 copy-start.5
  0.7 0.0 copy-start.1
  0.7 0.0 copy-start
  0.7 2.9 %forward.1 = (bf16[32,8,128]{2,1,0:T(8,128)(2,1)S(1)}, bf16[16,4,128,128]{3,2,1,0:T(8,128)(2,1)S(1)}) custom-call(s32[1,4,32]{2,1,0:T(4,128)} %bitcast.3, s32[1,32]{1,0:T(1,128)} %counts_ref.1, s32[1,6144]{1,0:T(1,128)} %nodes_hbm.1, bf16[4,16384]{1,0:T(4,128)(2,1)} %table_hbm.1, bf16[1,32,4,128,128]{4,3,2,1,0:T(8,128)(2,1)} %adj_hbm.3), custom_call_target="tpu_custom_call" | custom-call | tf_op jit(solution)/shard_map/forward/pallas_call | solution.py:236
  3.6 22.3 %all_to_all.20.x_ref = bf16[32,8,128]{2,1,0:T(8,128)(2,1)S(1)} all-to-all(bf16[32,8,128]{2,1,0:T(8,128)(2,1)S(1)} %get-tuple-element.16), channel_id=1, replica_groups=mesh['feat'=32,'rep'=16] {'feat'}, dimensions={0} | all-to-all | bytes 131072 | tf_op jit(solution)/shard_map/all_to_all | solution.py:258
  25.9 0.0 copy-done.2
  25.9 0.0 copy-done.5
  25.9 0.0 copy-done.1
  25.9 0.0 copy-done
  25.9 0.5 dense.1
  26.4 13.3 %all_to_all.21.got_ref = bf16[32,4,896]{2,1,0:T(4,128)(2,1)S(1)} all-to-all(bf16[32,4,896]{2,1,0:T(4,128)(2,1)S(1)} %get-tuple-element.17), channel_id=1, replica_groups=mesh['feat'=32,'rep'=16] {'feat'}, dimensions={0} | all-to-all | bytes 458752 | tf_op jit(solution)/shard_map/all_to_all | solution.py:270
  39.7 0.7 %feat_sum.1 = bf16[16,4,640]{2,1,0:T(4,128)(2,1)} custom-call(bf16[32,4,896]{2,1,0:T(4,128)(2,1)S(1)} %all_to_all.21.got_ref), custom_call_target="tpu_custom_call" | custom-call | tf_op jit(solution)/shard_map/feat_sum/pallas_call | solution.py:271
  40.4 10.5 %all-to-all-start.2 = ((bf16[16,4,640]{2,1,0:T(4,128)(2,1)}), bf16[16,4,640]{2,1,0:T(4,128)(2,1)S(1)}, u32[]{:S(2)}, u32[]{:S(2)}) async-start(bf16[16,4,640]{2,1,0:T(4,128)(2,1)} %feat_sum.1), calls=%async_computation.2 | async-start | bytes 163840 | tf_op jit(solution)/shard_map/all_to_all | solution.py:279
  50.9 0.0 copy-done.4
  50.9 0.0 copy-done.3
  50.9 4.0 %spread_back.1 = (bf16[1,4,6144]{2,1,0:T(4,128)(2,1)}, bf16[1,128,256]{2,1,0:T(8,128)(2,1)}) custom-call(s32[1,4,32]{2,1,0:T(4,128)S(1)} %bitcast.4, s32[1,32]{1,0:T(1,128)S(1)} %copy-done.4, bf16[32,4,896]{2,1,0:T(4,128)(2,1)S(1)} %all_to_all.21.got_ref, bf16[1,128,256]{2,1,0:T(8,128)(2,1)S(1)} %get-tuple-element.18.hid_ref, ...), custom_call_target="tpu_custom_call" | custom-call | flops 67108864 | bytes 4194304 | tf_op jit(solution)/shard_map/spread_back/pallas_call | solution.py:281
  54.9 4.2 %all-to-all-done.2.refs_0_ = bf16[16,4,640]{2,1,0:T(4,128)(2,1)S(1)} async-done(((bf16[16,4,640]{2,1,0:T(4,128)(2,1)}), bf16[16,4,640]{2,1,0:T(4,128)(2,1)S(1)}, u32[]{:S(2)}, u32[]{:S(2)}) %all-to-all-start.2) | async-done | bytes 81952 | tf_op jit(solution)/shard_map/all_to_all | solution.py:279
  59.1 13.1 %all_to_all.22.got_ref = bf16[32,4,512]{2,1,0:T(4,128)(2,1)S(1)} all-to-all(bf16[32,4,512]{2,1,0:T(4,128)(2,1)S(1)} %get-tuple-element.22), channel_id=1, replica_groups=mesh['feat'=32,'rep'=16] {'feat'}, dimensions={0} | all-to-all | bytes 262144 | tf_op jit(solution)/shard_map/all_to_all | solution.py:311
  72.2 0.7 %assemble.1 = (f32[128,256]{1,0:T(8,128)}, f32[128,256]{1,0:T(8,128)}, f32[1,256]{1,0:T(1,128)}) custom-call(bf16[32,4,512]{2,1,0:T(4,128)(2,1)S(1)} %all_to_all.22.got_ref, f32[1,256]{1,0:T(1,128)S(1)} %get-tuple-element.23.bias_ref), custom_call_target="tpu_custom_call" | custom-call | tf_op jit(solution)/shard_map/assemble/pallas_call | solution.py:312
  (1 shorter events, 0.0 us)
Async XLA Ops:
  0.6 50.3 %copy-start.4 = (s32[1,32]{1,0:T(1,128)S(1)}, s32[1,32]{1,0:T(1,128)}, u32[]{:S(2)}) copy-start(s32[1,32]{1,0:T(1,128)} %counts_ref.1) | copy-start | bytes 388
  0.6 50.3 %copy-start.3 = (s32[1,32,4]{1,2,0:T(4,128)S(1)}, s32[1,32,4]{1,2,0:T(4,128)}, u32[]{:S(2)}) copy-start(s32[1,32,4]{1,2,0:T(4,128)} %param.11) | copy-start | bytes 1540
  0.7 25.3 %copy-start.2 = (bf16[1,128,256]{2,1,0:T(8,128)(2,1)S(1)}, bf16[1,128,256]{2,1,0:T(8,128)(2,1)}, u32[]{:S(2)}) copy-start(bf16[1,128,256]{2,1,0:T(8,128)(2,1)} %cot_ref.1) | copy-start | bytes 196612
  0.7 25.3 %copy-start.5 = (f32[256]{0:T(256)S(1)}, f32[256]{0:T(256)}, u32[]{:S(2)}) copy-start(f32[256]{0:T(256)} %param.16) | copy-start | bytes 3076
  0.7 25.3 %copy-start.1 = (bf16[128,256]{1,0:T(8,128)(2,1)S(1)}, bf16[128,256]{1,0:T(8,128)(2,1)}, u32[]{:S(2)}) copy-start(bf16[128,256]{1,0:T(8,128)(2,1)} %nw_ref.1) | copy-start | bytes 196612
  0.7 25.3 %copy-start = (bf16[128,256]{1,0:T(8,128)(2,1)S(1)}, bf16[128,256]{1,0:T(8,128)(2,1)}, u32[]{:S(2)}) copy-start(bf16[128,256]{1,0:T(8,128)(2,1)} %sw_ref.1) | copy-start | bytes 196612
  40.4 18.6 %all-to-all-start.2 = ((bf16[16,4,640]{2,1,0:T(4,128)(2,1)}), bf16[16,4,640]{2,1,0:T(4,128)(2,1)S(1)}, u32[]{:S(2)}, u32[]{:S(2)}) async-start(bf16[16,4,640]{2,1,0:T(4,128)(2,1)} %feat_sum.1), calls=%async_computation.2 | async-start | bytes 163840 | tf_op jit(solution)/shard_map/all_to_all | solution.py:279

commit v7 on v6

--- a/solution.py
+++ b/solution.py
@@ -108,42 +108,29 @@
     )
     bias_sum = jnp.sum(grad_pre.astype(F32), axis=0, keepdims=True)
     half = hid // 2
-    tail = split_rows(bias_sum[:, :half], bias_sum[:, half:])
     peers = send_ref.shape[0]
     values = [back.reshape(peers, 8, rows)]
     values += [grads[:, at : at + half].reshape(peers, 8, half) for at in (0, half)]
-    parts = [v[:, at : at + 4] for v in values for at in (0, 4)]
-    parts.append(jnp.broadcast_to(tail[None], (peers, 4, half)))
+    parts = [v[:, at : at + 2] for v in values for at in (0, 2, 4, 6)]
+    tail = jnp.concatenate([bias_sum[:, :half], bias_sum[:, half:]], axis=0)
+    parts.append(jnp.broadcast_to(tail[None], (peers, 2, half)))
     send_ref[...] = jnp.concatenate(parts, axis=2).astype(BF16)
 
 
-def split_rows(first, second):
-    place = lax.broadcasted_iota(jnp.int32, (4, first.shape[1]), 0)
-    first_hi = first.astype(BF16).astype(F32)
-    second_hi = second.astype(BF16).astype(F32)
-    out = jnp.where(place == 0, first_hi, 0.0)
-    out = jnp.where(place == 1, second_hi, out)
-    out = jnp.where(place == 2, first - first_hi, out)
-    return jnp.where(place == 3, second - second_hi, out)
-
-
-def add_up(parts):
-    total = jnp.sum(parts, axis=0)
-    cols = total.shape[1] - 128
-    low = total[:, cols:]
-    return total[:, :cols], low[0:1] + low[2:3], low[1:2] + low[3:4]
-
-
 def feat_sum_kernel(got_ref, out_ref):
-    total, first, second = add_up(got_ref[...].astype(F32)[:, :, 256:])
-    whole = jnp.concatenate([total, split_rows(first, second)], axis=1).astype(BF16)
-    out_ref[...] = jnp.broadcast_to(whole[None], out_ref.shape)
+    total = jnp.sum(got_ref[...].astype(F32)[:, :, 512:], axis=0)
+    out_ref[...] = jnp.broadcast_to(total.astype(BF16)[None], out_ref.shape)
+
+
+def two_rows(value, at):
+    return jnp.concatenate([value[:, at : at + 128], value[:, at + 128 : at + 256]], axis=0)
 
 
 def rep_sum_kernel(factor, got_ref, after_ref, out_ref, bias_ref):
-    total, first, second = add_up(got_ref[...].astype(F32))
-    bias_ref[...] = factor * jnp.concatenate([first, second], axis=1)
-    out_ref[...] = jnp.broadcast_to((factor * total).astype(BF16)[None], out_ref.shape)
+    total = factor * jnp.sum(got_ref[...].astype(F32), axis=0)
+    bias_ref[...] = jnp.concatenate([total[0:1, 1024:], total[1:2, 1024:]], axis=1)
+    whole = jnp.concatenate([two_rows(total, at) for at in (0, 256, 512, 768)], axis=1)
+    out_ref[...] = jnp.broadcast_to(whole.astype(BF16)[None], out_ref.shape)
 
 
 def assemble_kernel(
@@ -181,7 +168,7 @@
             copy.wait()
         adj = held[b] if b < HELD else rest[b - HELD]
         count = counts_ref[0, b]
-        lhs = got_ref[b, :, side : 2 * side]
+        lhs = two_rows(got_ref[b].astype(F32), 2 * side).astype(BF16)
         contrib = lax.dot_general(
             lhs,
             adj.reshape(depth * side, side),
@@ -194,7 +181,7 @@
     for n in range(sources):
         total = acc[n]
         if n < blocks:
-            total = total + got_ref[n, :, 0:side].astype(F32)
+            total = total + two_rows(got_ref[n].astype(F32), 0)
         out_ref[0, :, n * side : (n + 1) * side] = total.astype(BF16)
 
 
@@ -260,7 +247,7 @@
         dense_kernel,
         out_shape=(
             jax.ShapeDtypeStruct(cotangent.shape, BF16),
-            jax.ShapeDtypeStruct((peers, chans, 7 * side), BF16),
+            jax.ShapeDtypeStruct((peers, 2, 13 * side), BF16),
         ),
         in_specs=[VMEM] * 5,
         out_specs=(VMEM, VMEM),
@@ -270,13 +257,16 @@
     got = lax.all_to_all(send, "feat", split_axis=0, concat_axis=0, tiled=True)
     partial = pl.pallas_call(
         feat_sum_kernel,
-        out_shape=jax.ShapeDtypeStruct((reps, chans, 5 * side), BF16),
+        out_shape=jax.ShapeDtypeStruct((reps, 2, 9 * side), BF16),
         in_specs=[VMEM],
         out_specs=VMEM,
         compiler_params=params(8),
         name="feat_sum",
     )(got)
-    over_rep = lax.all_to_all(partial, "rep", split_axis=0, concat_axis=0, tiled=True)
+    order = [2 * ((3 * y) % (reps // 2)) + core for y in range(reps // 2) for core in range(2)]
+    over_rep = lax.all_to_all(
+        partial, "rep", split_axis=0, concat_axis=0, tiled=True, axis_index_groups=[order]
+    )
     factor = float(rows * peers * reps) ** (-0.5)
     feature_grad, hidden = pl.pallas_call(
         backward_kernel,

time: 73.2 us -> 72.1 us (0.985)
  blocking collectives: 48.7 us -> 47.9 us
  transfers between devices with their start and end apart: 1 -> 1, of which waited for: 1 -> 1; matrix products, arithmetic and copies ran while one was open for 0% -> 0% of each run, Pallas kernels for 5% -> 6%
where the time goes in v7:
time: 72.1 us; the launch traced here: 71.8 us
  blocking collectives  47.9 us (66%)
  starting transfers between devices  10.5 us (15%)
  Pallas kernels  9.02 us (13%)
  waiting for transfers between devices  3.59 us (5%)
  between operations  0.73 us (1%)
    all_to_all x1, blocking collectives, local(): lax.all_to_all(sent, 'feat', split_axis=0, concat_axis=0, tiled=True)  22.3 us
    all_to_all x1, blocking collectives, local(): got = lax.all_to_all(send, 'feat', split_axis=0, concat_axis=0, tiled=True)  13.1 us
    all_to_all x1, blocking collectives, local(): lax.all_to_all(pieces, 'feat', split_axis=0, concat_axis=0, tiled=True)  12.4 us
    all_to_all x1, starting transfers between devices, local(): lax.all_to_all(partial, 'rep', split_axis=0, concat_axis=0, tiled=True, a...  10.5 us
    pallas_call x1, Pallas kernels, local(): pl.pallas_call(backward_kernel, out_shape=(jax.ShapeDtypeStruct((1, chans...  4.02 us
    all_to_all x1, waiting for transfers between devices, local(): lax.all_to_all(partial, 'rep', split_axis=0, concat_axis=0, tiled=True, a...  3.59 us
    pallas_call x1, Pallas kernels, local(): pl.pallas_call(forward_kernel, out_shape=(jax.ShapeDtypeStruct((peers, 8,...  2.88 us
  transfers between devices with their start and end apart: 1, of which 1 were waited for; matrix products, arithmetic and copies ran while one was open for 0% of the time, Pallas kernels for 6%

profile of v7, /device:TPU:1, one launch (start us, length us, event | category | flops | bytes accessed | tf_op | source)
XLA Modules:
  0.0 71.8 jit_solution(3084811047385492932)
XLA Ops:
  0.6 0.0 copy-start.4
  0.6 0.0 copy-start.3
  0.7 0.0 copy-start.2
  0.7 0.0 copy-start.5
  0.7 0.0 copy-start.1
  0.7 0.0 copy-start
  0.7 2.9 %forward.1 = (bf16[32,8,128]{2,1,0:T(8,128)(2,1)S(1)}, bf16[16,4,128,128]{3,2,1,0:T(8,128)(2,1)S(1)}) custom-call(s32[1,4,32]{2,1,0:T(4,128)} %bitcast.3, s32[1,32]{1,0:T(1,128)} %counts_ref.1, s32[1,6144]{1,0:T(1,128)} %nodes_hbm.1, bf16[4,16384]{1,0:T(4,128)(2,1)} %table_hbm.1, bf16[1,32,4,128,128]{4,3,2,1,0:T(8,128)(2,1)} %adj_hbm.3), custom_call_target="tpu_custom_call" | custom-call | tf_op jit(solution)/shard_map/forward/pallas_call | solution.py:223
  3.6 22.3 %all_to_all.20.x_ref = bf16[32,8,128]{2,1,0:T(8,128)(2,1)S(1)} all-to-all(bf16[32,8,128]{2,1,0:T(8,128)(2,1)S(1)} %get-tuple-element.16), channel_id=1, replica_groups=mesh['feat'=32,'rep'=16] {'feat'}, dimensions={0} | all-to-all | bytes 131072 | tf_op jit(solution)/shard_map/all_to_all | solution.py:245
  25.9 0.0 copy-done.2
  25.9 0.0 copy-done.5
  25.9 0.0 copy-done.1
  25.9 0.0 copy-done
  25.9 0.5 dense.1
  26.4 13.1 %all_to_all.21.got_ref = bf16[32,2,1664]{2,1,0:T(2,128)(2,1)S(1)} all-to-all(bf16[32,2,1664]{2,1,0:T(2,128)(2,1)S(1)} %get-tuple-element.17), channel_id=1, replica_groups=mesh['feat'=32,'rep'=16] {'feat'}, dimensions={0} | all-to-all | bytes 425984 | tf_op jit(solution)/shard_map/all_to_all | solution.py:257
  39.6 0.8 %feat_sum.1 = bf16[16,2,1152]{2,1,0:T(2,128)(2,1)} custom-call(bf16[32,2,1664]{2,1,0:T(2,128)(2,1)S(1)} %all_to_all.21.got_ref), custom_call_target="tpu_custom_call" | custom-call | tf_op jit(solution)/shard_map/feat_sum/pallas_call | solution.py:258
  40.4 10.5 %all-to-all-start.2 = ((bf16[16,2,1152]{2,1,0:T(2,128)(2,1)}), bf16[16,2,1152]{2,1,0:T(2,128)(2,1)S(1)}, u32[]{:S(2)}, u32[]{:S(2)}) async-start(bf16[16,2,1152]{2,1,0:T(2,128)(2,1)} %feat_sum.1), calls=%async_computation.2 | async-start | bytes 147456 | tf_op jit(solution)/shard_map/all_to_all | solution.py:267
  50.9 0.0 copy-done.4
  50.9 0.0 copy-done.3
  50.9 4.0 %spread_back.1 = (bf16[1,4,6144]{2,1,0:T(4,128)(2,1)}, bf16[1,128,256]{2,1,0:T(8,128)(2,1)}) custom-call(s32[1,4,32]{2,1,0:T(4,128)S(1)} %bitcast.4, s32[1,32]{1,0:T(1,128)S(1)} %copy-done.4, bf16[32,2,1664]{2,1,0:T(2,128)(2,1)S(1)} %all_to_all.21.got_ref, bf16[1,128,256]{2,1,0:T(8,128)(2,1)S(1)} %get-tuple-element.18.hid_ref, ...), custom_call_target="tpu_custom_call" | custom-call | flops 67108864 | bytes 4194304 | tf_op jit(solution)/shard_map/spread_back/pallas_call | solution.py:271
  54.9 3.6 %all-to-all-done.2.refs_0_ = bf16[16,2,1152]{2,1,0:T(2,128)(2,1)S(1)} async-done(((bf16[16,2,1152]{2,1,0:T(2,128)(2,1)}), bf16[16,2,1152]{2,1,0:T(2,128)(2,1)S(1)}, u32[]{:S(2)}, u32[]{:S(2)}) %all-to-all-start.2) | async-done | bytes 73760 | tf_op jit(solution)/shard_map/all_to_all | solution.py:267
  58.5 0.1 rep_sum.1
  58.6 12.4 %all_to_all.22.got_ref = bf16[32,4,512]{2,1,0:T(4,128)(2,1)S(1)} all-to-all(bf16[32,4,512]{2,1,0:T(4,128)(2,1)S(1)} %get-tuple-element.22), channel_id=1, replica_groups=mesh['feat'=32,'rep'=16] {'feat'}, dimensions={0} | all-to-all | bytes 262144 | tf_op jit(solution)/shard_map/all_to_all | solution.py:301
  71.0 0.7 %assemble.1 = (f32[128,256]{1,0:T(8,128)}, f32[128,256]{1,0:T(8,128)}, f32[1,256]{1,0:T(1,128)}) custom-call(bf16[32,4,512]{2,1,0:T(4,128)(2,1)S(1)} %all_to_all.22.got_ref, f32[1,256]{1,0:T(1,128)S(1)} %get-tuple-element.23.bias_ref), custom_call_target="tpu_custom_call" | custom-call | tf_op jit(solution)/shard_map/assemble/pallas_call | solution.py:302
Async XLA Ops:
  0.6 50.2 %copy-start.4 = (s32[1,32]{1,0:T(1,128)S(1)}, s32[1,32]{1,0:T(1,128)}, u32[]{:S(2)}) copy-start(s32[1,32]{1,0:T(1,128)} %counts_ref.1) | copy-start | bytes 388
  0.6 50.2 %copy-start.3 = (s32[1,32,4]{1,2,0:T(4,128)S(1)}, s32[1,32,4]{1,2,0:T(4,128)}, u32[]{:S(2)}) copy-start(s32[1,32,4]{1,2,0:T(4,128)} %param.11) | copy-start | bytes 1540
  0.7 25.3 %copy-start.2 = (bf16[1,128,256]{2,1,0:T(8,128)(2,1)S(1)}, bf16[1,128,256]{2,1,0:T(8,128)(2,1)}, u32[]{:S(2)}) copy-start(bf16[1,128,256]{2,1,0:T(8,128)(2,1)} %cot_ref.1) | copy-start | bytes 196612
  0.7 25.3 %copy-start.5 = (f32[256]{0:T(256)S(1)}, f32[256]{0:T(256)}, u32[]{:S(2)}) copy-start(f32[256]{0:T(256)} %param.16) | copy-start | bytes 3076
  0.7 25.3 %copy-start.1 = (bf16[128,256]{1,0:T(8,128)(2,1)S(1)}, bf16[128,256]{1,0:T(8,128)(2,1)}, u32[]{:S(2)}) copy-start(bf16[128,256]{1,0:T(8,128)(2,1)} %nw_ref.1) | copy-start | bytes 196612
  0.7 25.3 %copy-start = (bf16[128,256]{1,0:T(8,128)(2,1)S(1)}, bf16[128,256]{1,0:T(8,128)(2,1)}, u32[]{:S(2)}) copy-start(bf16[128,256]{1,0:T(8,128)(2,1)} %sw_ref.1) | copy-start | bytes 196612
  40.4 18.1 %all-to-all-start.2 = ((bf16[16,2,1152]{2,1,0:T(2,128)(2,1)}), bf16[16,2,1152]{2,1,0:T(2,128)(2,1)S(1)}, u32[]{:S(2)}, u32[]{:S(2)}) async-start(bf16[16,2,1152]{2,1,0:T(2,128)(2,1)} %feat_sum.1), calls=%async_computation.2 | async-start | bytes 147456 | tf_op jit(solution)/shard_map/all_to_all | solution.py:267

commit v8 on v7

--- a/solution.py
+++ b/solution.py
@@ -8,6 +8,7 @@
 F32 = jnp.float32
 BF16 = jnp.bfloat16
 HELD = 16
+FEAT_ORDER = [4 * ((3 * z) % 8) + x for z in range(8) for x in range(4)]
 LOW = 256
 CHUNK = 512
 
@@ -82,7 +83,7 @@
         ]
         lhs = jnp.concatenate(picked, axis=1).astype(BF16)
         agg = jnp.dot(lhs, adj.reshape(depth * side, side), preferred_element_type=F32)
-        staged[b] = jnp.where(upper, feats[b], agg)
+        staged[FEAT_ORDER.index(b)] = jnp.where(upper, feats[b], agg)
     out_ref[...] = staged[...].astype(BF16)
 
 
@@ -94,7 +95,9 @@
     upper = lax.broadcasted_iota(jnp.int32, sw.shape, 1) < 4
     even = jnp.where(upper, sw, pltpu.roll(nw, 4, 1))
     odd = jnp.where(upper, pltpu.roll(sw, 4, 1), nw)
-    weight = jnp.concatenate([even, odd], axis=1).reshape(2 * feats, hid).astype(BF16)
+    weight = jnp.concatenate([even, odd], axis=1).reshape(feats // 4, 8, hid)
+    weight = jnp.concatenate([weight[i : i + 1] for i in FEAT_ORDER], axis=0)
+    weight = weight.reshape(2 * feats, hid).astype(BF16)
     rows = x_ref.shape[2]
     x = x_ref[...].reshape(2 * feats, rows)
     preact = lax.dot_general(x, weight, (((0,), (0,)), ((), ())), preferred_element_type=F32)
@@ -168,7 +171,7 @@
             copy.wait()
         adj = held[b] if b < HELD else rest[b - HELD]
         count = counts_ref[0, b]
-        lhs = two_rows(got_ref[b].astype(F32), 2 * side).astype(BF16)
+        lhs = two_rows(got_ref[FEAT_ORDER.index(b)].astype(F32), 2 * side).astype(BF16)
         contrib = lax.dot_general(
             lhs,
             adj.reshape(depth * side, side),
@@ -181,7 +184,7 @@
     for n in range(sources):
         total = acc[n]
         if n < blocks:
-            total = total + two_rows(got_ref[n].astype(F32), 0)
+            total = total + two_rows(got_ref[FEAT_ORDER.index(n)].astype(F32), 0)
         out_ref[0, :, n * side : (n + 1) * side] = total.astype(BF16)
 
 
@@ -242,7 +245,9 @@
         compiler_params=params(24),
         name="forward",
     )(*[in_hbm(v) for v in (lists, block_counts, node_ids, feature_table, adjacency)])
-    arrived = lax.all_to_all(sent, "feat", split_axis=0, concat_axis=0, tiled=True)
+    arrived = lax.all_to_all(
+        sent, "feat", split_axis=0, concat_axis=0, tiled=True, axis_index_groups=[FEAT_ORDER]
+    )
     hid_vmem, send = pl.pallas_call(
         dense_kernel,
         out_shape=(
@@ -254,7 +259,9 @@
         compiler_params=params(16),
         name="dense",
     )(arrived, self_weight, neigh_weight, bias_vector.reshape(1, hid), cotangent)
-    got = lax.all_to_all(send, "feat", split_axis=0, concat_axis=0, tiled=True)
+    got = lax.all_to_all(
+        send, "feat", split_axis=0, concat_axis=0, tiled=True, axis_index_groups=[FEAT_ORDER]
+    )
     partial = pl.pallas_call(
         feat_sum_kernel,
         out_shape=jax.ShapeDtypeStruct((reps, 2, 9 * side), BF16),

time: 72.1 us -> 72.1 us (level)
  no operation moved by 1% of the time
where the time goes in v8:
time: 72.1 us; the launch traced here: 71.8 us
  blocking collectives  47.9 us (66%)
  starting transfers between devices  10.5 us (15%)
  Pallas kernels  9.02 us (13%)
  waiting for transfers between devices  3.59 us (5%)
  between operations  0.73 us (1%)
    all_to_all x1, blocking collectives, local(): lax.all_to_all(sent, 'feat', split_axis=0, concat_axis=0, tiled=True, axi...  22.3 us
    all_to_all x1, blocking collectives, local(): lax.all_to_all(send, 'feat', split_axis=0, concat_axis=0, tiled=True, axi...  13.1 us
    all_to_all x1, blocking collectives, local(): lax.all_to_all(pieces, 'feat', split_axis=0, concat_axis=0, tiled=True)  12.4 us
    all_to_all x1, starting transfers between devices, local(): lax.all_to_all(partial, 'rep', split_axis=0, concat_axis=0, tiled=True, a...  10.5 us
    pallas_call x1, Pallas kernels, local(): pl.pallas_call(backward_kernel, out_shape=(jax.ShapeDtypeStruct((1, chans...  4.02 us
    all_to_all x1, waiting for transfers between devices, local(): lax.all_to_all(partial, 'rep', split_axis=0, concat_axis=0, tiled=True, a...  3.59 us
    pallas_call x1, Pallas kernels, local(): pl.pallas_call(forward_kernel, out_shape=(jax.ShapeDtypeStruct((peers, 8,...  2.89 us
  transfers between devices with their start and end apart: 1, of which 1 were waited for; matrix products, arithmetic and copies ran while one was open for 0% of the time, Pallas kernels for 6%

profile of v8, /device:TPU:1, one launch (start us, length us, event | category | flops | bytes accessed | tf_op | source)
XLA Modules:
  0.0 71.8 jit_solution(2099040580331865198)
XLA Ops:
  0.6 0.0 copy-start.4
  0.6 0.0 copy-start.3
  0.7 0.0 copy-start.2
  0.7 0.0 copy-start.5
  0.7 0.0 copy-start.1
  0.7 0.0 copy-start
  0.7 2.9 %forward.1 = (bf16[32,8,128]{2,1,0:T(8,128)(2,1)S(1)}, bf16[16,4,128,128]{3,2,1,0:T(8,128)(2,1)S(1)}) custom-call(s32[1,4,32]{2,1,0:T(4,128)} %bitcast.3, s32[1,32]{1,0:T(1,128)} %counts_ref.1, s32[1,6144]{1,0:T(1,128)} %nodes_hbm.1, bf16[4,16384]{1,0:T(4,128)(2,1)} %table_hbm.1, bf16[1,32,4,128,128]{4,3,2,1,0:T(8,128)(2,1)} %adj_hbm.3), custom_call_target="tpu_custom_call" | custom-call | tf_op jit(solution)/shard_map/forward/pallas_call | solution.py:226
  3.6 22.3 %all_to_all.20.x_ref = bf16[32,8,128]{2,1,0:T(8,128)(2,1)S(1)} all-to-all(bf16[32,8,128]{2,1,0:T(8,128)(2,1)S(1)} %get-tuple-element.16), channel_id=1, replica_groups={{0,16,32,48,192,208,224,240,384,400,416,432,64,80,96,112,256,272,288,30..., dimensions={0} | all-to-all | bytes 131072 | tf_op jit(solution)/shard_map/all_to_all | solution.py:248
  25.9 0.0 copy-done.2
  25.9 0.0 copy-done.5
  25.9 0.0 copy-done.1
  25.9 0.0 copy-done
  25.9 0.5 dense.1
  26.4 13.1 %all_to_all.21.got_ref = bf16[32,2,1664]{2,1,0:T(2,128)(2,1)S(1)} all-to-all(bf16[32,2,1664]{2,1,0:T(2,128)(2,1)S(1)} %get-tuple-element.17), channel_id=1, replica_groups={{0,16,32,48,192,208,224,240,384,400,416,432,64,80,96,112,256,272,288,30..., dimensions={0} | all-to-all | bytes 425984 | tf_op jit(solution)/shard_map/all_to_all | solution.py:262
  39.5 0.8 %feat_sum.1 = bf16[16,2,1152]{2,1,0:T(2,128)(2,1)} custom-call(bf16[32,2,1664]{2,1,0:T(2,128)(2,1)S(1)} %all_to_all.21.got_ref), custom_call_target="tpu_custom_call" | custom-call | tf_op jit(solution)/shard_map/feat_sum/pallas_call | solution.py:265
  40.3 10.5 %all-to-all-start.2 = ((bf16[16,2,1152]{2,1,0:T(2,128)(2,1)}), bf16[16,2,1152]{2,1,0:T(2,128)(2,1)S(1)}, u32[]{:S(2)}, u32[]{:S(2)}) async-start(bf16[16,2,1152]{2,1,0:T(2,128)(2,1)} %feat_sum.1), calls=%async_computation.2 | async-start | bytes 147456 | tf_op jit(solution)/shard_map/all_to_all | solution.py:274
  50.9 0.0 copy-done.4
  50.9 0.0 copy-done.3
  50.9 4.0 %spread_back.1 = (bf16[1,4,6144]{2,1,0:T(4,128)(2,1)}, bf16[1,128,256]{2,1,0:T(8,128)(2,1)}) custom-call(s32[1,4,32]{2,1,0:T(4,128)S(1)} %bitcast.4, s32[1,32]{1,0:T(1,128)S(1)} %copy-done.4, bf16[32,2,1664]{2,1,0:T(2,128)(2,1)S(1)} %all_to_all.21.got_ref, bf16[1,128,256]{2,1,0:T(8,128)(2,1)S(1)} %get-tuple-element.18.hid_ref, ...), custom_call_target="tpu_custom_call" | custom-call | flops 67108864 | bytes 4194304 | tf_op jit(solution)/shard_map/spread_back/pallas_call | solution.py:278
  54.9 3.6 %all-to-all-done.2.refs_0_ = bf16[16,2,1152]{2,1,0:T(2,128)(2,1)S(1)} async-done(((bf16[16,2,1152]{2,1,0:T(2,128)(2,1)}), bf16[16,2,1152]{2,1,0:T(2,128)(2,1)S(1)}, u32[]{:S(2)}, u32[]{:S(2)}) %all-to-all-start.2) | async-done | bytes 73760 | tf_op jit(solution)/shard_map/all_to_all | solution.py:274
  58.5 0.1 rep_sum.1
  58.6 12.4 %all_to_all.22.got_ref = bf16[32,4,512]{2,1,0:T(4,128)(2,1)S(1)} all-to-all(bf16[32,4,512]{2,1,0:T(4,128)(2,1)S(1)} %get-tuple-element.22), channel_id=1, replica_groups=mesh['feat'=32,'rep'=16] {'feat'}, dimensions={0} | all-to-all | bytes 262144 | tf_op jit(solution)/shard_map/all_to_all | solution.py:308
  71.0 0.7 %assemble.1 = (f32[128,256]{1,0:T(8,128)}, f32[128,256]{1,0:T(8,128)}, f32[1,256]{1,0:T(1,128)}) custom-call(bf16[32,4,512]{2,1,0:T(4,128)(2,1)S(1)} %all_to_all.22.got_ref, f32[1,256]{1,0:T(1,128)S(1)} %get-tuple-element.23.bias_ref), custom_call_target="tpu_custom_call" | custom-call | tf_op jit(solution)/shard_map/assemble/pallas_call | solution.py:309
Async XLA Ops:
  0.6 50.2 %copy-start.4 = (s32[1,32]{1,0:T(1,128)S(1)}, s32[1,32]{1,0:T(1,128)}, u32[]{:S(2)}) copy-start(s32[1,32]{1,0:T(1,128)} %counts_ref.1) | copy-start | bytes 388
  0.6 50.2 %copy-start.3 = (s32[1,32,4]{1,2,0:T(4,128)S(1)}, s32[1,32,4]{1,2,0:T(4,128)}, u32[]{:S(2)}) copy-start(s32[1,32,4]{1,2,0:T(4,128)} %param.11) | copy-start | bytes 1540
  0.7 25.3 %copy-start.2 = (bf16[1,128,256]{2,1,0:T(8,128)(2,1)S(1)}, bf16[1,128,256]{2,1,0:T(8,128)(2,1)}, u32[]{:S(2)}) copy-start(bf16[1,128,256]{2,1,0:T(8,128)(2,1)} %cot_ref.1) | copy-start | bytes 196612
  0.7 25.3 %copy-start.5 = (f32[256]{0:T(256)S(1)}, f32[256]{0:T(256)}, u32[]{:S(2)}) copy-start(f32[256]{0:T(256)} %param.16) | copy-start | bytes 3076
  0.7 25.3 %copy-start.1 = (bf16[128,256]{1,0:T(8,128)(2,1)S(1)}, bf16[128,256]{1,0:T(8,128)(2,1)}, u32[]{:S(2)}) copy-start(bf16[128,256]{1,0:T(8,128)(2,1)} %nw_ref.1) | copy-start | bytes 196612
  0.7 25.2 %copy-start = (bf16[128,256]{1,0:T(8,128)(2,1)S(1)}, bf16[128,256]{1,0:T(8,128)(2,1)}, u32[]{:S(2)}) copy-start(bf16[128,256]{1,0:T(8,128)(2,1)} %sw_ref.1) | copy-start | bytes 196612
  40.3 18.2 %all-to-all-start.2 = ((bf16[16,2,1152]{2,1,0:T(2,128)(2,1)}), bf16[16,2,1152]{2,1,0:T(2,128)(2,1)S(1)}, u32[]{:S(2)}, u32[]{:S(2)}) async-start(bf16[16,2,1152]{2,1,0:T(2,128)(2,1)} %feat_sum.1), calls=%async_computation.2 | async-start | bytes 147456 | tf_op jit(solution)/shard_map/all_to_all | solution.py:274
